TPU v7x, 512 devices: a whole 4x8x8 slice. The times are simulated.
512 devices in a mesh: rep: 32 (over x_hi, y, core), fsdp: 16 (over z, x_lo).
Axes of the slice: x: 4 (x_hi: 2, x_lo: 2; x = x_hi * 2 + x_lo), y: 8, z: 8, core: 2. Of those that a mesh axis runs over, the one named last changes fastest.
Arguments:
- tokens: bfloat16 [98304, 4096], P(('rep', 'fsdp')), may hold values from -6 to 6
- norm_gain: float32 [32, 4096], P('rep'), may hold values from 0.25 to 1.75
- doc_ids: int32 [32, 3072], P('rep', 'fsdp'), may hold values from 0 to 7, never falling along the last dimension, each value on 1 to 768 neighbouring positions
- key_cotangent: bfloat16 [98304, 512], P(('rep', 'fsdp')), may hold values from -6 to 6
- numerator: float32 [32, 4096, 512], P('rep', 'fsdp'), may hold values from -6 to 6
- first_moment: float32 [32, 4096, 512], P('rep', 'fsdp'), may hold values from -4 to 4
- second_moment: float32 [32, 4096, 512], P('rep', 'fsdp'), may hold values from 0.05 to 2
- push_weight: float32 [32], P('rep'), may hold values from 0.5 to 2
- gossip_step: int32 [1], replicated, may hold values from 0 to 63
Outputs:
- keys: bfloat16 [98304, 512], P(('rep', 'fsdp'))
- numerator_new: float32 [32, 4096, 512], P('rep', 'fsdp')
- first_new: float32 [32, 4096, 512], P('rep', 'fsdp')
- second_new: float32 [32, 4096, 512], P('rep', 'fsdp')
- weight_new: float32 [32], P('rep')
Inputs may be any that keep to these rules, and one draw needn't show every extreme that they name: `doc_ids`: within each replica's row the ids never fall; each of the 8 documents has 1 to 768 tokens, and one has exactly 768.
All inputs are finite; a program needn't handle non-finite values.
Results may differ from a plain program's by a relative error of at most 0.006.
Values may be sent and summed in bfloat16 or wider, within the bound.
No kernel may reach another device: no remote copies, remote signals or barrier semaphores. Data moves between devices by JAX's collectives and lax.ppermute only.
A program may use at most 64 MiB of HBM per device.

v0:
```python
from functools import partial

import jax
import jax.numpy as jnp
from jax import lax
from jax.sharding import PartitionSpec as P

D = 4096
KVH = 4
HD = 128
DOCS = 8
KW = 512


THETA = 1000000.0
BETA_ONE = 0.9
BETA_TWO = 0.95
STEP_RATE = 0.1
WEIGHT_DECAY = 0.2
EPSILON = 1e-08
NORM_EPSILON = 1e-05
FIRST_CORRECTION = 1.0 - 0.9**10
SECOND_CORRECTION = 1.0 - 0.95**10


def as_sent(x):

    def short(part):
        return part.astype(jnp.bfloat16) if part.dtype == jnp.float32 else part

    return jax.tree.map(short, x)


def from_behind(block, axis, distance):
    devices = range(lax.axis_size(axis))
    route = [((i - distance) % len(devices), i) for i in devices]
    return lax.ppermute(block, axis, route)


def rotate_half(values):
    return jnp.concatenate([-values[..., HD // 2 :], values[..., : HD // 2]], axis=-1)


def rotary_tables(positions):
    frequency = THETA ** (-(jnp.arange(HD // 2, dtype=jnp.float32) * 2.0 / HD))
    angles = positions.astype(jnp.float32)[:, None] * frequency[None, :]
    cosine = jnp.concatenate([jnp.cos(angles), jnp.cos(angles)], axis=-1)[:, None, :]
    sine = jnp.concatenate([jnp.sin(angles), jnp.sin(angles)], axis=-1)[:, None, :]
    return (cosine, sine)


def push_by(distance, shard_values, weight_values):
    return (
        from_behind(as_sent(shard_values), "rep", distance).astype(shard_values.dtype),
        from_behind(as_sent(weight_values), "rep", distance).astype(weight_values.dtype),
    )


def local(
    tokens,
    norm_gain,
    doc_ids,
    key_cotangent,
    numerator,
    first_moment,
    second_moment,
    push_weight,
    gossip_step,
):
    token_count = tokens.shape[0]
    weight = push_weight[0]
    token_values = tokens.astype(jnp.float32)
    stats = jnp.mean(token_values * token_values, axis=-1, keepdims=True)
    normed = (token_values * lax.rsqrt(stats + NORM_EPSILON) * norm_gain[0][None, :]).astype(
        jnp.bfloat16
    )
    model = (numerator[0] / weight).astype(jnp.bfloat16)
    local_ids = doc_ids[0]
    onehot = (local_ids[:, None] == jnp.arange(DOCS, dtype=jnp.int32)[None, :]).astype(jnp.int32)
    counts = jnp.sum(onehot, axis=0)
    local_index = jnp.arange(token_count, dtype=jnp.int32)
    totals = lax.psum(counts, "fsdp")
    starts = jnp.cumsum(totals) - totals
    offset = lax.axis_index("fsdp") * token_count
    positions = offset + local_index - jnp.sum(onehot * starts[None, :], axis=1)
    cosine, sine = rotary_tables(positions)
    columns = normed
    projected = jnp.dot(
        columns,
        lax.all_gather(model, "fsdp", axis=0, tiled=True),
        preferred_element_type=jnp.float32,
    )
    pre = (projected * D ** (-0.5)).reshape(token_count, KVH, HD)
    keys = (pre * cosine + rotate_half(pre) * sine).reshape(token_count, KW).astype(jnp.bfloat16)
    cotangent = key_cotangent.astype(jnp.float32).reshape(token_count, KVH, HD)
    back = (
        ((cotangent * cosine - rotate_half(cotangent * sine)) * D ** (-0.5))
        .reshape(token_count, KW)
        .astype(jnp.bfloat16)
    )
    columns = normed
    grad = lax.psum_scatter(
        lax.dot_general(
            columns, back, (((0,), (0,)), ((), ())), preferred_element_type=jnp.float32
        ).astype(jnp.bfloat16),
        "fsdp",
        scatter_dimension=0,
        tiled=True,
    ).astype(jnp.float32)
    shard = numerator[0]
    first_new = BETA_ONE * first_moment[0] + (1.0 - BETA_ONE) * grad
    second_new = BETA_TWO * second_moment[0] + (1.0 - BETA_TWO) * grad * grad
    update = first_new / FIRST_CORRECTION / (jnp.sqrt(second_new / SECOND_CORRECTION) + EPSILON)
    half = shard - STEP_RATE * (update + WEIGHT_DECAY * (shard / weight))
    sent = 0.5 * half[None]
    sent_weight = 0.5 * push_weight
    bit_count = lax.axis_size("rep").bit_length() - 1
    branches = [partial(push_by, 1 << exponent) for exponent in range(bit_count)]
    received, received_weight = lax.switch(gossip_step[0] % bit_count, branches, sent, sent_weight)
    numerator_new = sent + received
    weight_new = sent_weight + received_weight
    return (keys, numerator_new, first_new[None], second_new[None], weight_new)


def solution(mesh):
    in_specs = (
        P(("rep", "fsdp"), None),
        P("rep", None),
        P("rep", "fsdp"),
        P(("rep", "fsdp"), None),
        P("rep", "fsdp", None),
        P("rep", "fsdp", None),
        P("rep", "fsdp", None),
        P("rep"),
        P(),
    )
    out_specs = (
        P(("rep", "fsdp"), None),
        P("rep", "fsdp", None),
        P("rep", "fsdp", None),
        P("rep", "fsdp", None),
        P("rep"),
    )
    return jax.shard_map(local, mesh=mesh, in_specs=in_specs, out_specs=out_specs, check_vma=False)
```

profile of v0, /device:TPU:16, one launch (start us, length us, event | category | flops | bytes accessed | tf_op | source)
XLA Modules:
  0.0 260.1 jit_solution(1675318811349507325)
XLA Ops:
  7.2 0.0 reduce-scatter.2.cloned.1.call-start
  7.2 0.0 copy-start
  7.2 0.0 copy-start.2
  7.3 0.0 copy-start.3
  7.3 1.9 fusion
  9.2 0.8 convert_reduce_fusion
  10.0 1.1 reshape.86
  11.1 22.0 %psum.7 = s32[8]{0:T(128)S(1)} all-reduce(s32[8]{0:T(128)S(1)} %convert_reduce_fusion), channel_id=1, replica_groups=mesh['rep'=32,'fsdp'=16] {'fsdp'}, use_global_device_ids=true, to_apply=%region_2.0 | all-reduce | flops 8 | bytes 64 | tf_op jit(solution)/shard_map/psum | solution.py:82
  33.0 0.2 reduce-window.9
  33.2 0.8 select_reduce_fusion
  34.0 0.4 multiply_cosine_fusion
  34.4 0.1 pad_maximum_fusion.1
  34.5 0.1 broadcast_multiply_fusion
  34.6 0.3 slice_negate_fusion
  34.9 0.3 pad_maximum_fusion
  35.2 0.1 mul.160
  35.3 0.0 copy-done
  35.3 0.0 copy-done.2
  35.3 0.0 copy-done.3
  35.3 3.4 %convolution_convert_fusion = bf16[4096,512]{1,0:T(8,128)(2,1)} fusion(bf16[192,4096]{1,0:T(8,128)(2,1)S(1)} %copy-done, f32[4096]{0:T(1024)S(1)} %bitcast.66, f32[192]{0:T(256)S(1)} %add_rsqrt_fusion, f32[24,8,4,128]{3,2,1,0:T(4,128)S(1)} %bitcast.63, f32[24,8,4,128]{3,2,1,0:T(4,128)S(1)} %bitcast.60, bf16[192,512]{1,0:T(8,128)(2,1)S(1)} %copy-done.2), kind=kOutput, calls=%fused_computation | convolution fusion | flops 811040768 | bytes 6767360 | tf_op jit(solution)/shard_map/dot_general | solution.py:103
  38.7 0.0 copy-start.1
  38.7 0.0 reduce-scatter.2.cloned.1.call-update
  38.7 0.0 all-gather.2.cloned.1.call-start
  39.4 98.9 %reduce-scatter.2.cloned.1.call-done = bf16[256,512]{1,0:T(8,128)(2,1)} async-done(((bf16[4096,512]{1,0:T(8,128)(2,1)}), bf16[256,512]{1,0:T(8,128)(2,1)}) %reduce-scatter.2.cloned.1.call-update) | async-done | bytes 262160 | tf_op jit(solution)/shard_map/reduce_scatter | solution.py:102
  138.3 0.0 copy-done.1
  138.3 2.7 %fusion.13 = (f32[1,256,512]{2,1,0:T(8,128)}, f32[1,256,512]{2,1,0:T(8,128)S(1)}, f32[1,256,512]{2,1,0:T(8,128)}, bf16[256,512]{1,0:T(8,128)(2,1)}) fusion(bf16[256,512]{1,0:T(8,128)(2,1)} %reduce-scatter.2.cloned.1.call-done, f32[1,256,512]{2,1,0:T(8,128)S(1)} %copy-done.1, f32[]{:T(128)} %bitcast.59, f32[1,256,512]{2,1,0:T(8,128)} %param.19, ...), kind=kLoop, calls=%fused_computation.27 | loop fusion | flops 2490368 | bytes 3670020 | tf_op jit(solution)/shard_map/broadcast_in_dim | solution.py:122
  141.0 0.0 all-gather.2.cloned.1.call-update
  141.7 22.7 %conditional.4 = (f32[1,256,512]{2,1,0:T(8,128)S(1)}, f32[1]{0:T(128)}) conditional(s32[]{:T(128)} %clamp.3, (f32[1,256,512]{2,1,0:T(8,128)S(1)}, f32[1]{0:T(128)}) %tuple.60, (f32[1,256,512]{2,1,0:T(8,128)S(1)}, f32[1]{0:T(128)}) %tuple.60, (f32[1,256,512]{2,1,0:T(8,128)S(1)}, f32[1]{0:T(128)}) %tuple.60, ...), branch_computations={%region_6.7_spmd, %region_7.8_spmd, %region_8.9_spmd, %region_9.10... | conditional | flops 262146 | bytes 2621556
  141.8 5.6 %collective-permute-start.6 = (bf16[1,256,512]{2,1,0:T(8,128)(2,1)S(1)}, bf16[1,256,512]{2,1,0:T(8,128)(2,1)S(1)}, u32[]{:S(2)}, u32[]{:S(2)}) collective-permute-start(bf16[1,256,512]{2,1,0:T(8,128)(2,1)S(1)} %convert_element_type.100), channel_id=1, source_target_pairs={{384,0},{400,16},{416,32},{432,48},{448,64},{464,80},{480,96},{496... | collective-permute-start | bytes 786440 | tf_op jit(solution)/shard_map/cond/branch_3_fun/ppermute | solution.py:37
  147.4 9.0 %collective-permute-start.7 = (bf16[1]{0:T(256)(128)(2,1)}, bf16[1]{0:T(256)(128)(2,1)}, u32[]{:S(2)}, u32[]{:S(2)}) collective-permute-start(bf16[1]{0:T(256)(128)(2,1)} %convert_element_type.102), channel_id=1, source_target_pairs={{384,0},{400,16},{416,32},{432,48},{448,64},{464,80},{480,96},{496... | collective-permute-start | bytes 14 | tf_op jit(solution)/shard_map/cond/branch_3_fun/ppermute | solution.py:37
  156.3 7.3 %collective-permute-done.7 = bf16[1]{0:T(256)(128)(2,1)} collective-permute-done((bf16[1]{0:T(256)(128)(2,1)}, bf16[1]{0:T(256)(128)(2,1)}, u32[]{:S(2)}, u32[]{:S(2)}) %collective-permute-start.7) | collective-permute-done | bytes 34 | tf_op jit(solution)/shard_map/cond/branch_3_fun/ppermute | solution.py:37
  164.3 0.0 collective-permute-done.6
  164.3 0.1 convert_element_type.133
  164.4 0.9 add.65
  165.3 82.2 %all-gather.2.cloned.1.call-done = bf16[4096,512]{1,0:T(8,128)(2,1)} async-done(((bf16[256,512]{1,0:T(8,128)(2,1)}), bf16[4096,512]{1,0:T(8,128)(2,1)}) %all-gather.2.cloned.1.call-update) | async-done | bytes 4194320 | tf_op jit(solution)/shard_map/all_gather | solution.py:90
  247.4 3.2 %convolution_multiply_fusion = f32[192,512]{1,0:T(8,128)S(1)} fusion(bf16[4096,512]{1,0:T(8,128)(2,1)} %all-gather.2.cloned.1.call-done, bf16[192,4096]{1,0:T(8,128)(2,1)S(1)} %copy-done, f32[4096]{0:T(1024)S(1)} %bitcast.67, f32[192]{0:T(256)S(1)} %add_rsqrt_fusion), kind=kOutput, calls=%fused_computation.6 | convolution fusion | flops 808550400 | bytes 6177536 | tf_op jit(solution)/shard_map/dot_general | solution.py:88
  250.7 0.1 reshape.85
  250.8 0.3 slice_negate_fusion.1
  251.1 0.3 maximum_multiply_fusion
  251.4 0.8 fusion.11
  (5 shorter events, 0.1 us)
Async XLA Ops:
  7.2 131.2 %reduce-scatter.2.cloned.1.call-start = ((), (), s32[]{:S(2)}) async-start(), calls=%async_computation.2 | async-start | bytes 4456448 | tf_op jit(solution)/shard_map/reduce_scatter | solution.py:102
  7.2 28.0 %copy-start = (bf16[192,4096]{1,0:T(8,128)(2,1)S(1)}, bf16[192,4096]{1,0:T(8,128)(2,1)}, u32[]{:S(2)}) copy-start(bf16[192,4096]{1,0:T(8,128)(2,1)} %param.14) | copy-start | bytes 4718596
  7.2 28.0 %copy-start.2 = (bf16[192,512]{1,0:T(8,128)(2,1)S(1)}, bf16[192,512]{1,0:T(8,128)(2,1)}, u32[]{:S(2)}) copy-start(bf16[192,512]{1,0:T(8,128)(2,1)} %param.17) | copy-start | bytes 589828
  7.3 28.0 %copy-start.3 = (f32[1,4096]{1,0:T(1,128)S(1)}, f32[1,4096]{1,0:T(1,128)}, u32[]{:S(2)}) copy-start(f32[1,4096]{1,0:T(1,128)} %param.15) | copy-start | bytes 49156
  38.7 99.7 %copy-start.1 = (f32[1,256,512]{2,1,0:T(8,128)S(1)}, f32[1,256,512]{2,1,0:T(8,128)}, u32[]{:S(2)}) copy-start(f32[1,256,512]{2,1,0:T(8,128)} %param.20) | copy-start | bytes 1572868
  38.7 208.7 %all-gather.2.cloned.1.call-start = ((), (), s32[]{:S(2)}) async-start(), calls=%async_computation.1 | async-start | bytes 4456448 | tf_op jit(solution)/shard_map/all_gather | solution.py:90
  141.8 22.5 %collective-permute-start.6 = (bf16[1,256,512]{2,1,0:T(8,128)(2,1)S(1)}, bf16[1,256,512]{2,1,0:T(8,128)(2,1)S(1)}, u32[]{:S(2)}, u32[]{:S(2)}) collective-permute-start(bf16[1,256,512]{2,1,0:T(8,128)(2,1)S(1)} %convert_element_type.100), channel_id=1, source_target_pairs={{384,0},{400,16},{416,32},{432,48},{448,64},{464,80},{480,96},{496... | collective-permute-start | bytes 786440 | tf_op jit(solution)/shard_map/cond/branch_3_fun/ppermute | solution.py:37
  147.4 16.3 %collective-permute-start.7 = (bf16[1]{0:T(256)(128)(2,1)}, bf16[1]{0:T(256)(128)(2,1)}, u32[]{:S(2)}, u32[]{:S(2)}) collective-permute-start(bf16[1]{0:T(256)(128)(2,1)} %convert_element_type.102), channel_id=1, source_target_pairs={{384,0},{400,16},{416,32},{432,48},{448,64},{464,80},{480,96},{496... | collective-permute-start | bytes 14 | tf_op jit(solution)/shard_map/cond/branch_3_fun/ppermute | solution.py:37
Sparse Core Ops, SparseCore 0:
  38.8 99.4 reduce-scatter.1
  141.2 106.2 all-gather.1
where the time goes:
time: 260 us
  waiting for transfers between devices  188 us (72%)
  blocking collectives  22 us (8%)
  between operations  16.7 us (6%)
  starting transfers between devices  14.6 us (6%)
  other arithmetic  9.85 us (4%)
  matrix products  6.58 us (3%)
    reduce_scatter x1, waiting for transfers between devices, local(): lax.psum_scatter(lax.dot_general(columns, back, (((0,), (0,)), ((), ())),...  98.9 us
    all_gather x1, waiting for transfers between devices, local(): lax.all_gather(model, 'fsdp', axis=0, tiled=True)  82.2 us
    psum x1, blocking collectives, local(): totals = lax.psum(counts, 'fsdp')  22 us
    ppermute x2, starting transfers between devices, from_behind(): return lax.ppermute(block, axis, route)  14.5 us
    ppermute x2, waiting for transfers between devices, from_behind(): return lax.ppermute(block, axis, route)  7.34 us
  transfers between devices with their start and end apart: 4, of which 3 were waited for; matrix products, arithmetic and copies ran while one was open for 0% of the time, Pallas kernels for 0%

commit v1 on v0

v1 whole, which is shorter than its diff:
```python
from functools import partial

import jax
import jax.numpy as jnp
from jax import lax
from jax.experimental import pallas as pl
from jax.experimental.pallas import tpu as pltpu
from jax.sharding import PartitionSpec as P

D = 4096
KVH = 4
HD = 128
DOCS = 8
KW = 512
TOK = 192
NZ = 8
ROWS = 256
HALF = NZ * ROWS


THETA = 1000000.0
BETA_ONE = 0.9
BETA_TWO = 0.95
STEP_RATE = 0.1
WEIGHT_DECAY = 0.2
EPSILON = 1e-08
NORM_EPSILON = 1e-05
FIRST_CORRECTION = 1.0 - 0.9**10
SECOND_CORRECTION = 1.0 - 0.95**10
SCALE = D ** (-0.5)

PARAMS = pltpu.CompilerParams(vmem_limit_bytes=32 * 1024 * 1024)
F32, BF16 = jnp.float32, jnp.bfloat16


def along_z(value, distance):
    route = [(f, ((f // 2 + distance) % NZ) * 2 + f % 2) for f in range(2 * NZ)]
    return lax.ppermute(value, "fsdp", route)


def swap_x(value):
    return lax.ppermute(value, "fsdp", [(f, f ^ 1) for f in range(2 * NZ)])


def norm_kernel(place, tokens, gain, cotangent, keep, send):
    z, x = place[0], place[1]
    send[:, HALF:] = cotangent[...]

    def rows_of(i, carry):
        rows = pl.ds(pl.multiple_of(i * 16, 16), 16)
        values = tokens[rows, :].astype(F32)
        scale = lax.rsqrt(jnp.mean(values * values, axis=-1, keepdims=True) + NORM_EPSILON)
        for o in range(NZ):
            for side, target in ((x, keep), (1 - x, send)):
                columns = pl.ds(pl.multiple_of((2 * lax.rem(z + o, NZ) + side) * ROWS, ROWS), ROWS)
                part = tokens[rows, columns].astype(F32) * scale * gain[:, columns]
                target[rows, o * ROWS : (o + 1) * ROWS] = part.astype(BF16)
        return carry

    lax.fori_loop(0, TOK // 16, rows_of, 0)


def normalise(place, tokens, gain, cotangent):
    return pl.pallas_call(
        norm_kernel,
        out_shape=(
            jax.ShapeDtypeStruct((TOK, HALF), BF16),
            jax.ShapeDtypeStruct((TOK, HALF + KW), BF16),
        ),
        in_specs=[pl.BlockSpec(memory_space=pltpu.SMEM)] + [pl.BlockSpec(memory_space=pltpu.VMEM)] * 3,
        out_specs=[pl.BlockSpec(memory_space=pltpu.VMEM)] * 2,
        compiler_params=PARAMS,
        cost_estimate=pl.CostEstimate(flops=8 * TOK * D, bytes_accessed=4 * TOK * D, transcendentals=0),
        name="normalise",
    )(place, tokens, gain, cotangent)


def rotate_rows(cotangent, cosine, sine):
    parts = []
    for h in range(KVH):
        y = cotangent[:, h * HD : (h + 1) * HD].astype(F32)
        s = y * sine
        turned = jnp.concatenate([-s[:, HD // 2 :], s[:, : HD // 2]], axis=-1)
        parts.append(((y * cosine - turned) * SCALE).astype(BF16))
    return jnp.concatenate(parts, axis=-1)


def grad_kernel(keep, recv, cotangent, cosine, sine, up_one, down_one, up_two, down_two, own, back):
    back[:TOK] = rotate_rows(cotangent[...], cosine[:TOK], sine[:TOK])
    back[TOK:] = rotate_rows(recv[:, HALF:], cosine[TOK:], sine[TOK:])
    over = (((0,), (0,)), ((), ()))

    def block(o):
        columns = slice(o * ROWS, (o + 1) * ROWS)
        return lax.dot_general(keep[:, columns], back[:TOK], over, preferred_element_type=F32) + lax.dot_general(
            recv[:, columns], back[TOK:], over, preferred_element_type=F32
        )

    half = block(4).astype(BF16)
    up_two[...] = half[: ROWS // 2]
    down_two[...] = half[ROWS // 2 :]
    up_one[:ROWS] = block(3).astype(BF16)
    down_one[:ROWS] = block(5).astype(BF16)
    up_one[ROWS:] = block(1).astype(BF16)
    down_one[ROWS:] = block(7).astype(BF16)
    own[:ROWS] = block(0)
    own[ROWS : 2 * ROWS] = block(2)
    own[2 * ROWS :] = block(6)


def grad_parts(keep, recv, cotangent, cosine, sine):
    shape = jax.ShapeDtypeStruct
    return pl.pallas_call(
        grad_kernel,
        out_shape=(
            shape((2 * ROWS, KW), BF16),
            shape((2 * ROWS, KW), BF16),
            shape((ROWS // 2, KW), BF16),
            shape((ROWS // 2, KW), BF16),
            shape((3 * ROWS, KW), F32),
        ),
        in_specs=[pl.BlockSpec(memory_space=pltpu.VMEM)] * 5,
        out_specs=[pl.BlockSpec(memory_space=pltpu.VMEM)] * 5,
        scratch_shapes=[pltpu.VMEM((2 * TOK, KW), BF16)],
        compiler_params=PARAMS,
        cost_estimate=pl.CostEstimate(flops=4 * TOK * HALF * KW, bytes_accessed=6 << 20, transcendentals=0),
        name="grad_parts",
    )(keep, recv, cotangent, cosine, sine)


def keys_kernel(place, keep, recv, model, own, other):
    z = place[0]

    def half_of(values):
        total = jnp.zeros((TOK, KW), F32)
        for o in range(NZ):
            rows = pl.ds(pl.multiple_of(lax.rem(z + o, NZ) * ROWS, ROWS), ROWS)
            total = total + jnp.dot(
                values[:, o * ROWS : (o + 1) * ROWS], model[rows, :], preferred_element_type=F32
            )
        return total

    other[...] = half_of(recv).astype(BF16)
    own[...] = half_of(keep)


def keys_parts(place, keep, recv, model):
    return pl.pallas_call(
        keys_kernel,
        out_shape=(jax.ShapeDtypeStruct((TOK, KW), F32), jax.ShapeDtypeStruct((TOK, KW), BF16)),
        in_specs=[pl.BlockSpec(memory_space=pltpu.SMEM)] + [pl.BlockSpec(memory_space=pltpu.VMEM)] * 3,
        out_specs=[pl.BlockSpec(memory_space=pltpu.VMEM)] * 2,
        compiler_params=PARAMS,
        cost_estimate=pl.CostEstimate(flops=4 * TOK * HALF * KW, bytes_accessed=5 << 20, transcendentals=0),
        name="keys_parts",
    )(place, keep, recv, model)


def push_by(distance, values):
    n = lax.axis_size("rep")
    return lax.ppermute(values, "rep", [((i - distance) % n, i) for i in range(n)])


def local(
    tokens,
    norm_gain,
    doc_ids,
    key_cotangent,
    numerator,
    first_moment,
    second_moment,
    push_weight,
    gossip_step,
):
    f = lax.axis_index("fsdp")
    z, x = f // 2, f % 2
    place = jnp.stack([z, x]).astype(jnp.int32)
    weight = push_weight[0]

    other_ids = swap_x(doc_ids)
    keep, send = normalise(place, tokens, norm_gain, key_cotangent)
    recv = swap_x(send)

    model = (numerator[0] / weight).astype(BF16)
    zs = [[2 * i + side for i in range(NZ)] for side in range(2)]
    models = lax.all_gather(model, "fsdp", axis=0, axis_index_groups=zs, tiled=True)

    ids = jnp.concatenate([doc_ids[0], other_ids[0]])
    documents = jnp.arange(DOCS, dtype=jnp.int32)[None, :]
    counts = jnp.sum((ids[:, None] == documents).astype(jnp.int32), axis=0, keepdims=True)
    behind_one, behind_two = along_z(counts, 1), along_z(counts, 2)
    before = jnp.where(z >= 1, behind_one, 0) + jnp.where(z >= 2, behind_two, 0)
    row = jnp.arange(TOK, dtype=jnp.int32)
    index = jnp.concatenate([x * TOK + row, (1 - x) * TOK + row])
    shift = jnp.where(ids[:, None] == documents, before, 0) - jnp.where(ids[:, None] > documents, counts, 0)
    positions = index + jnp.sum(shift, axis=1)
    frequency = THETA ** (-(jnp.arange(HD // 2, dtype=jnp.float32) * 2.0 / HD))
    frequency = jnp.concatenate([frequency, frequency])
    angles = positions.astype(jnp.float32)[:, None] * frequency[None, :]
    cosine, sine = jnp.cos(angles), jnp.sin(angles)

    up_one, down_one, up_two, down_two, own = grad_parts(keep, recv, key_cotangent, cosine, sine)
    up_one, down_one = along_z(up_one, 1), along_z(down_one, -1)
    up_two, down_two = along_z(up_two, 2), along_z(down_two, -2)
    zero = jnp.zeros((ROWS // 2, KW), F32)
    up = own[ROWS : 2 * ROWS] + up_one[:ROWS] + jnp.concatenate([up_two.astype(F32), zero])
    down = own[2 * ROWS :] + down_one[:ROWS] + jnp.concatenate([zero, down_two.astype(F32)])
    up, down = along_z(up.astype(BF16), 2), along_z(down.astype(BF16), -2)
    near = own[:ROWS] + up_one[ROWS:] + down_one[ROWS:]

    own_keys, other_keys = keys_parts(place, keep, recv, models)
    pre = (own_keys + swap_x(other_keys).astype(F32)) * SCALE
    pre = pre.reshape(TOK, KVH, HD)
    turned = jnp.concatenate([-pre[..., HD // 2 :], pre[..., : HD // 2]], axis=-1)
    keys = pre * cosine[:TOK, None, :] + turned * sine[:TOK, None, :]
    keys = keys.reshape(TOK, KW).astype(BF16)

    grad = near + up.astype(F32) + down.astype(F32)
    shard = numerator[0]
    first_new = BETA_ONE * first_moment[0] + (1.0 - BETA_ONE) * grad
    second_new = BETA_TWO * second_moment[0] + (1.0 - BETA_TWO) * grad * grad
    update = first_new / FIRST_CORRECTION / (jnp.sqrt(second_new / SECOND_CORRECTION) + EPSILON)
    half = shard - STEP_RATE * (update + WEIGHT_DECAY * (shard / weight))
    sent = 0.5 * half
    sent_weight = 0.5 * push_weight
    message = jnp.concatenate([sent, jnp.broadcast_to(sent_weight[:, None], (16, KW))]).astype(BF16)
    bit_count = lax.axis_size("rep").bit_length() - 1
    branches = [partial(push_by, 1 << exponent) for exponent in range(bit_count)]
    received = lax.switch(gossip_step[0] % bit_count, branches, message)
    numerator_new = sent + received[:ROWS]
    weight_new = sent_weight + received[ROWS, :1]
    return (keys, numerator_new[None], first_new[None], second_new[None], weight_new)


def solution(mesh):
    in_specs = (
        P(("rep", "fsdp"), None),
        P("rep", None),
        P("rep", "fsdp"),
        P(("rep", "fsdp"), None),
        P("rep", "fsdp", None),
        P("rep", "fsdp", None),
        P("rep", "fsdp", None),
        P("rep"),
        P(),
    )
    out_specs = (
        P(("rep", "fsdp"), None),
        P("rep", "fsdp", None),
        P("rep", "fsdp", None),
        P("rep", "fsdp", None),
        P("rep"),
    )
    return jax.shard_map(local, mesh=mesh, in_specs=in_specs, out_specs=out_specs, check_vma=False)
```

time: 260 us -> 165 us (0.63)
  the two profiles are of different devices: /device:TPU:16 before, /device:TPU:2 now
where the time goes in v1:
time: 165 us; the launch traced here: 164 us
  waiting for transfers between devices  78 us (47%)
  starting transfers between devices  49.9 us (30%)
  between operations  17.4 us (11%)
  other arithmetic  7.02 us (4%)
  local copies, waits for them, and re-layouts  6.09 us (4%)
  Pallas kernels  5.6 us (3%)
    ppermute x8, starting transfers between devices, along_z(): return lax.ppermute(value, 'fsdp', route)  34.2 us
    all_gather x1, waiting for transfers between devices, local(): lax.all_gather(model, 'fsdp', axis=0, axis_index_groups=zs, tiled=True)  29.5 us
    ppermute x8, waiting for transfers between devices, along_z(): return lax.ppermute(value, 'fsdp', route)  21 us
    ppermute x3, waiting for transfers between devices, swap_x(): return lax.ppermute(value, 'fsdp', [(f, f ^ 1) for f in range(2 * NZ)])  18.8 us
    ppermute x3, starting transfers between devices, swap_x(): return lax.ppermute(value, 'fsdp', [(f, f ^ 1) for f in range(2 * NZ)])  12.2 us
    ppermute x1, waiting for transfers between devices, push_by(): lax.ppermute(values, 'rep', [((i - distance) % n, i) for i in range(n)])  8.66 us
    unnamed x18, local copies, waits for them, and re-layouts  4.67 us
    ppermute x1, starting transfers between devices, push_by(): lax.ppermute(values, 'rep', [((i - distance) % n, i) for i in range(n)])  3.49 us
  transfers between devices with their start and end apart: 13, of which 10 were waited for; matrix products, arithmetic and copies ran while one was open for 3% of the time, Pallas kernels for 0%

profile of v1, /device:TPU:2, one launch (start us, length us, event | category | flops | bytes accessed | tf_op | source)
XLA Modules:
  0.0 164.1 jit_solution(15366824859072262832)
XLA Ops:
  7.2 0.1 pad_add_fusion.1.place
  7.3 1.4 copy-done.1
  8.7 0.9 copy-done.2
  9.7 0.7 copy-done.4
  10.4 2.3 %normalise.1 = (bf16[192,2048]{1,0:T(8,128)(2,1)S(1)}, bf16[192,2560]{1,0:T(8,128)(2,1)S(1)}) custom-call(s32[2]{0:T(128)S(1)} %pad_add_fusion.1.place, bf16[192,4096]{1,0:T(8,128)(2,1)S(1)} %copy-done.1, f32[1,4096]{1,0:T(1,128)S(1)} %copy-done.4, bf16[192,512]{1,0:T(8,128)(2,1)S(1)} %copy-done.2), custom_call_target="tpu_custom_call" | custom-call | flops 6291456 | bytes 3145728 | tf_op jit(solution)/shard_map/normalise/pallas_call | solution.py:64
  12.7 7.8 %collective-permute-start.5 = (bf16[192,2560]{1,0:T(8,128)(2,1)S(1)}, bf16[192,2560]{1,0:T(8,128)(2,1)S(1)}, u32[]{:S(2)}, u32[]{:S(2)}) collective-permute-start(bf16[192,2560]{1,0:T(8,128)(2,1)S(1)} %get-tuple-element.26), channel_id=1, source_target_pairs={{0,1},{1,0},{2,3},{3,2},{4,5},{5,4},{6,7},{7,6},{8,9},{9,8},{10,11... | collective-permute-start | bytes 2949128 | tf_op jit(solution)/shard_map/ppermute | solution.py:42
  20.6 1.9 %collective-permute-start.7 = (s32[1,192]{1,0:T(1,128)S(1)}, s32[1,192]{1,0:T(1,128)S(1)}, u32[]{:S(2)}, u32[]{:S(2)}) collective-permute-start(s32[1,192]{1,0:T(1,128)S(1)} %copy-done.8), channel_id=1, source_target_pairs={{0,1},{1,0},{2,3},{3,2},{4,5},{5,4},{6,7},{7,6},{8,9},{9,8},{10,11... | collective-permute-start | bytes 2312 | tf_op jit(solution)/shard_map/ppermute | solution.py:42
  22.5 0.1 pad_maximum_fusion
  22.6 15.6 %collective-permute-done.7 = s32[1,192]{1,0:T(1,128)S(1)} collective-permute-done((s32[1,192]{1,0:T(1,128)S(1)}, s32[1,192]{1,0:T(1,128)S(1)}, u32[]{:S(2)}, u32[]{:S(2)}) %collective-permute-start.7) | collective-permute-done | bytes 800 | tf_op jit(solution)/shard_map/ppermute | solution.py:42
  38.2 0.1 pad_add_fusion
  38.2 0.1 convert_reduce_fusion
  38.4 4.3 %collective-permute-start.8 = (s32[1,8]{1,0:T(1,128)S(1)}, s32[1,8]{1,0:T(1,128)S(1)}, u32[]{:S(2)}, u32[]{:S(2)}) collective-permute-start(s32[1,8]{1,0:T(1,128)S(1)} %bitcast.59), channel_id=1, source_target_pairs={{0,2},{1,3},{2,4},{3,5},{4,6},{5,7},{6,8},{7,9},{8,10},{9,11},{10,... | collective-permute-start | bytes 104 | tf_op jit(solution)/shard_map/ppermute | solution.py:38
  42.6 6.1 %collective-permute-start.9 = (s32[1,8]{1,0:T(1,128)S(1)}, s32[1,8]{1,0:T(1,128)S(1)}, u32[]{:S(2)}, u32[]{:S(2)}) collective-permute-start(s32[1,8]{1,0:T(1,128)S(1)} %bitcast.60), channel_id=1, source_target_pairs={{0,4},{1,5},{2,6},{3,7},{4,8},{5,9},{6,10},{7,11},{8,12},{9,13},{1... | collective-permute-start | bytes 104 | tf_op jit(solution)/shard_map/ppermute | solution.py:38
  48.7 2.1 %collective-permute-done.8 = s32[1,8]{1,0:T(1,128)S(1)} collective-permute-done((s32[1,8]{1,0:T(1,128)S(1)}, s32[1,8]{1,0:T(1,128)S(1)}, u32[]{:S(2)}, u32[]{:S(2)}) %collective-permute-start.8) | collective-permute-done | bytes 64 | tf_op jit(solution)/shard_map/ppermute | solution.py:38
  50.8 3.4 %collective-permute-done.9 = s32[1,8]{1,0:T(1,128)S(1)} collective-permute-done((s32[1,8]{1,0:T(1,128)S(1)}, s32[1,8]{1,0:T(1,128)S(1)}, u32[]{:S(2)}, u32[]{:S(2)}) %collective-permute-start.9) | collective-permute-done | bytes 64 | tf_op jit(solution)/shard_map/ppermute | solution.py:38
  54.2 0.1 subtract_reduce_fusion
  54.3 0.1 fusion.6
  54.4 0.8 multiply_cosine_fusion
  55.2 1.7 %grad_parts.1 = (bf16[512,512]{1,0:T(8,128)(2,1)S(1)}, bf16[512,512]{1,0:T(8,128)(2,1)S(1)}, bf16[128,512]{1,0:T(8,128)(2,1)S(1)}, bf16[128,512]{1,0:T(8,128)(2,1)S(1)}, f32[768,512]{1,0:T(8,128)S(1)}) custom-call(bf16[192,2048]{1,0:T(8,128)(2,1)S(1)} %get-tuple-element.25.keep, bf16[192,2560]{1,0:T(8,128)(2,1)S(1)} %collective-permute-done.5.recv, ...), custom_call_target="tpu_custom_call" | custom-call | flops 805306368 | bytes 6291456 | tf_op jit(solution)/shard_map/grad_parts/pallas_call | solution.py:113
  56.9 2.1 %collective-permute-start.10 = (bf16[512,512]{1,0:T(8,128)(2,1)S(1)}, bf16[512,512]{1,0:T(8,128)(2,1)S(1)}, u32[]{:S(2)}, u32[]{:S(2)}) collective-permute-start(bf16[512,512]{1,0:T(8,128)(2,1)S(1)} %get-tuple-element.30), channel_id=1, source_target_pairs={{0,2},{1,3},{2,4},{3,5},{4,6},{5,7},{6,8},{7,9},{8,10},{9,11},{10,... | collective-permute-start | bytes 1572872 | tf_op jit(solution)/shard_map/ppermute | solution.py:38
  58.9 5.1 %collective-permute-start.11 = (bf16[512,512]{1,0:T(8,128)(2,1)S(1)}, bf16[512,512]{1,0:T(8,128)(2,1)S(1)}, u32[]{:S(2)}, u32[]{:S(2)}) collective-permute-start(bf16[512,512]{1,0:T(8,128)(2,1)S(1)} %get-tuple-element.31), channel_id=1, source_target_pairs={{0,14},{1,15},{2,0},{3,1},{4,2},{5,3},{6,4},{7,5},{8,6},{9,7},{10,... | collective-permute-start | bytes 1572872 | tf_op jit(solution)/shard_map/ppermute | solution.py:38
  64.1 1.9 %collective-permute-start.12 = (bf16[128,512]{1,0:T(8,128)(2,1)S(1)}, bf16[128,512]{1,0:T(8,128)(2,1)S(1)}, u32[]{:S(2)}, u32[]{:S(2)}) collective-permute-start(bf16[128,512]{1,0:T(8,128)(2,1)S(1)} %get-tuple-element.32), channel_id=1, source_target_pairs={{0,4},{1,5},{2,6},{3,7},{4,8},{5,9},{6,10},{7,11},{8,12},{9,13},{1... | collective-permute-start | bytes 393224 | tf_op jit(solution)/shard_map/ppermute | solution.py:38
  66.0 6.0 %collective-permute-start.14 = (bf16[128,512]{1,0:T(8,128)(2,1)S(1)}, bf16[128,512]{1,0:T(8,128)(2,1)S(1)}, u32[]{:S(2)}, u32[]{:S(2)}) collective-permute-start(bf16[128,512]{1,0:T(8,128)(2,1)S(1)} %get-tuple-element.33), channel_id=1, source_target_pairs={{0,12},{1,13},{2,14},{3,15},{4,0},{5,1},{6,2},{7,3},{8,4},{9,5},{1... | collective-permute-start | bytes 393224 | tf_op jit(solution)/shard_map/ppermute | solution.py:38
  72.1 4.9 %collective-permute-done.12 = bf16[128,512]{1,0:T(8,128)(2,1)S(1)} collective-permute-done((bf16[128,512]{1,0:T(8,128)(2,1)S(1)}, bf16[128,512]{1,0:T(8,128)(2,1)S(1)}, u32[]{:S(2)}, u32[]{:S(2)}) %collective-permute-start.12) | collective-permute-done | bytes 131104 | tf_op jit(solution)/shard_map/ppermute | solution.py:38
  77.0 1.5 collective-permute-done.14
  78.5 0.2 add_convert_fusion.1
  78.7 6.6 %collective-permute-start.15 = (bf16[256,512]{1,0:T(8,128)(2,1)S(1)}, bf16[256,512]{1,0:T(8,128)(2,1)S(1)}, u32[]{:S(2)}, u32[]{:S(2)}) collective-permute-start(bf16[256,512]{1,0:T(8,128)(2,1)S(1)} %get-tuple-element.54), channel_id=1, source_target_pairs={{0,12},{1,13},{2,14},{3,15},{4,0},{5,1},{6,2},{7,3},{8,4},{9,5},{1... | collective-permute-start | bytes 786440 | tf_op jit(solution)/shard_map/ppermute | solution.py:38
  85.3 2.1 %collective-permute-start.13 = (bf16[256,512]{1,0:T(8,128)(2,1)S(1)}, bf16[256,512]{1,0:T(8,128)(2,1)S(1)}, u32[]{:S(2)}, u32[]{:S(2)}) collective-permute-start(bf16[256,512]{1,0:T(8,128)(2,1)S(1)} %get-tuple-element.53), channel_id=1, source_target_pairs={{0,4},{1,5},{2,6},{3,7},{4,8},{5,9},{6,10},{7,11},{8,12},{9,13},{1... | collective-permute-start | bytes 786440 | tf_op jit(solution)/shard_map/ppermute | solution.py:38
  88.1 4.5 %collective-permute-done.15 = bf16[256,512]{1,0:T(8,128)(2,1)S(1)} collective-permute-done((bf16[256,512]{1,0:T(8,128)(2,1)S(1)}, bf16[256,512]{1,0:T(8,128)(2,1)S(1)}, u32[]{:S(2)}, u32[]{:S(2)}) %collective-permute-start.15) | collective-permute-done | bytes 262176 | tf_op jit(solution)/shard_map/ppermute | solution.py:38
  92.6 4.6 %collective-permute-done.13 = bf16[256,512]{1,0:T(8,128)(2,1)S(1)} collective-permute-done((bf16[256,512]{1,0:T(8,128)(2,1)S(1)}, bf16[256,512]{1,0:T(8,128)(2,1)S(1)}, u32[]{:S(2)}, u32[]{:S(2)}) %collective-permute-start.13) | collective-permute-done | bytes 262176 | tf_op jit(solution)/shard_map/ppermute | solution.py:38
  97.2 1.0 fusion.5
  98.2 1.3 fusion.9
  100.3 12.2 %conditional.1 = (bf16[272,512]{1,0:T(8,128)(2,1)}) conditional(s32[]{:T(128)} %clamp.3, (bf16[256,512]{1,0:T(8,128)(2,1)S(1)}, bf16[1]{0:T(256)(128)(2,1)}) %tuple.24, (bf16[256,512]{1,0:T(8,128)(2,1)S(1)}, bf16[1]{0:T(256)(128)(2,1)}) %tuple.24, (bf16[256,512]{1,0:T(8,128)(2,1)S(1)}, ...), branch_computations={%region_2.3_spmd, %region_3.4_spmd, %region_4.5_spmd, %region_5.6_... | conditional | bytes 1654834 | solution.py:229
  100.3 3.5 %collective-permute-start.1 = (bf16[272,512]{1,0:T(8,128)(2,1)S(1)}, bf16[272,512]{1,0:T(8,128)(2,1)}, u32[]{:S(2)}, u32[]{:S(2)}) collective-permute-start(bf16[272,512]{1,0:T(8,128)(2,1)S(1)} %concatenate.44), channel_id=1, source_target_pairs={{480,0},{496,16},{0,32},{16,48},{32,64},{48,80},{64,96},{80,112},{... | collective-permute-start | bytes 835592 | tf_op jit(solution)/shard_map/cond/branch_1_fun/ppermute | solution.py:161
  103.8 8.7 %collective-permute-done.1 = bf16[272,512]{1,0:T(8,128)(2,1)} collective-permute-done((bf16[272,512]{1,0:T(8,128)(2,1)S(1)}, bf16[272,512]{1,0:T(8,128)(2,1)}, u32[]{:S(2)}, u32[]{:S(2)}) %collective-permute-start.1) | collective-permute-done | bytes 278560 | tf_op jit(solution)/shard_map/cond/branch_1_fun/ppermute | solution.py:161
  112.5 1.2 slice.61
  114.3 29.5 %all-gather.2.cloned.1.call-done.model = bf16[2048,512]{1,0:T(8,128)(2,1)} async-done(((bf16[256,512]{1,0:T(8,128)(2,1)}), bf16[2048,512]{1,0:T(8,128)(2,1)}) %all-gather.2.cloned.1.call-update) | async-done | bytes 2097168 | tf_op jit(solution)/shard_map/all_gather | solution.py:186
  143.8 1.6 copy-done
  145.4 1.5 keys_parts.1
  146.9 2.5 %collective-permute-start.6 = (bf16[192,512]{1,0:T(8,128)(2,1)S(1)}, bf16[192,512]{1,0:T(8,128)(2,1)S(1)}, u32[]{:S(2)}, u32[]{:S(2)}) collective-permute-start(bf16[192,512]{1,0:T(8,128)(2,1)S(1)} %get-tuple-element.28), channel_id=1, source_target_pairs={{0,1},{1,0},{2,3},{3,2},{4,5},{5,4},{6,7},{7,6},{8,9},{9,8},{10,11... | collective-permute-start | bytes 589832 | tf_op jit(solution)/shard_map/ppermute | solution.py:42
  149.4 1.8 %add_bitcast_fusion = f32[1,256,512]{2,1,0:T(8,128)} fusion(f32[256,512]{1,0:T(8,128)S(1)} %get-tuple-element.52, bf16[272,512]{1,0:T(8,128)(2,1)} %get-tuple-element.63), kind=kLoop, calls=%fused_computation.6 | loop fusion | flops 262144 | bytes 1310720 | tf_op jit(solution)/shard_map/broadcast_in_dim | solution.py:232
  151.2 3.3 %collective-permute-done.6 = bf16[192,512]{1,0:T(8,128)(2,1)S(1)} collective-permute-done((bf16[192,512]{1,0:T(8,128)(2,1)S(1)}, bf16[192,512]{1,0:T(8,128)(2,1)S(1)}, u32[]{:S(2)}, u32[]{:S(2)}) %collective-permute-start.6) | collective-permute-done | bytes 196640 | tf_op jit(solution)/shard_map/ppermute | solution.py:42
  154.5 0.1 add_multiply_fusion
  154.5 0.1 reshape.48
  154.7 0.3 slice_negate_fusion
  155.0 0.3 maximum_multiply_fusion
  155.2 0.1 mul.105
  155.3 0.8 fusion.2
  (25 shorter events, 0.2 us)
Async XLA Ops:
  7.2 13.4 %copy-start.8 = (s32[1,192]{1,0:T(1,128)S(1)}, s32[1,192]{1,0:T(1,128)}, u32[]{:S(2)}) copy-start(s32[1,192]{1,0:T(1,128)} %param.16) | copy-start | bytes 2308
  7.2 136.6 %all-gather.2.cloned.1.call-start = ((), (), s32[]{:S(2)}) async-start(), calls=%async_computation | async-start | bytes 2359296 | tf_op jit(solution)/shard_map/all_gather | solution.py:186
  7.3 1.4 copy-start.1
  8.7 0.9 copy-start.2
  9.7 0.7 copy-start.4
  10.4 44.8 %copy-start.3 = (bf16[192,512]{1,0:T(8,128)(2,1)S(1)}, bf16[192,512]{1,0:T(8,128)(2,1)}, u32[]{:S(2)}) copy-start(bf16[192,512]{1,0:T(8,128)(2,1)} %cotangent.3) | copy-start | bytes 589828
  12.7 42.4 %collective-permute-start.5 = (bf16[192,2560]{1,0:T(8,128)(2,1)S(1)}, bf16[192,2560]{1,0:T(8,128)(2,1)S(1)}, u32[]{:S(2)}, u32[]{:S(2)}) collective-permute-start(bf16[192,2560]{1,0:T(8,128)(2,1)S(1)} %get-tuple-element.26), channel_id=1, source_target_pairs={{0,1},{1,0},{2,3},{3,2},{4,5},{5,4},{6,7},{7,6},{8,9},{9,8},{10,11... | collective-permute-start | bytes 2949128 | tf_op jit(solution)/shard_map/ppermute | solution.py:42
  20.6 17.6 %collective-permute-start.7 = (s32[1,192]{1,0:T(1,128)S(1)}, s32[1,192]{1,0:T(1,128)S(1)}, u32[]{:S(2)}, u32[]{:S(2)}) collective-permute-start(s32[1,192]{1,0:T(1,128)S(1)} %copy-done.8), channel_id=1, source_target_pairs={{0,1},{1,0},{2,3},{3,2},{4,5},{5,4},{6,7},{7,6},{8,9},{9,8},{10,11... | collective-permute-start | bytes 2312 | tf_op jit(solution)/shard_map/ppermute | solution.py:42
  38.4 12.5 %collective-permute-start.8 = (s32[1,8]{1,0:T(1,128)S(1)}, s32[1,8]{1,0:T(1,128)S(1)}, u32[]{:S(2)}, u32[]{:S(2)}) collective-permute-start(s32[1,8]{1,0:T(1,128)S(1)} %bitcast.59), channel_id=1, source_target_pairs={{0,2},{1,3},{2,4},{3,5},{4,6},{5,7},{6,8},{7,9},{8,10},{9,11},{10,... | collective-permute-start | bytes 104 | tf_op jit(solution)/shard_map/ppermute | solution.py:38
  42.6 11.6 %collective-permute-start.9 = (s32[1,8]{1,0:T(1,128)S(1)}, s32[1,8]{1,0:T(1,128)S(1)}, u32[]{:S(2)}, u32[]{:S(2)}) collective-permute-start(s32[1,8]{1,0:T(1,128)S(1)} %bitcast.60), channel_id=1, source_target_pairs={{0,4},{1,5},{2,6},{3,7},{4,8},{5,9},{6,10},{7,11},{8,12},{9,13},{1... | collective-permute-start | bytes 104 | tf_op jit(solution)/shard_map/ppermute | solution.py:38
  56.9 40.3 %copy-start.5 = (f32[1,256,512]{2,1,0:T(8,128)S(1)}, f32[1,256,512]{2,1,0:T(8,128)}, u32[]{:S(2)}) copy-start(f32[1,256,512]{2,1,0:T(8,128)} %param.20) | copy-start | bytes 1572868
  56.9 21.6 %collective-permute-start.10 = (bf16[512,512]{1,0:T(8,128)(2,1)S(1)}, bf16[512,512]{1,0:T(8,128)(2,1)S(1)}, u32[]{:S(2)}, u32[]{:S(2)}) collective-permute-start(bf16[512,512]{1,0:T(8,128)(2,1)S(1)} %get-tuple-element.30), channel_id=1, source_target_pairs={{0,2},{1,3},{2,4},{3,5},{4,6},{5,7},{6,8},{7,9},{8,10},{9,11},{10,... | collective-permute-start | bytes 1572872 | tf_op jit(solution)/shard_map/ppermute | solution.py:38
  58.9 19.6 %collective-permute-start.11 = (bf16[512,512]{1,0:T(8,128)(2,1)S(1)}, bf16[512,512]{1,0:T(8,128)(2,1)S(1)}, u32[]{:S(2)}, u32[]{:S(2)}) collective-permute-start(bf16[512,512]{1,0:T(8,128)(2,1)S(1)} %get-tuple-element.31), channel_id=1, source_target_pairs={{0,14},{1,15},{2,0},{3,1},{4,2},{5,3},{6,4},{7,5},{8,6},{9,7},{10,... | collective-permute-start | bytes 1572872 | tf_op jit(solution)/shard_map/ppermute | solution.py:38
  64.1 12.9 %collective-permute-start.12 = (bf16[128,512]{1,0:T(8,128)(2,1)S(1)}, bf16[128,512]{1,0:T(8,128)(2,1)S(1)}, u32[]{:S(2)}, u32[]{:S(2)}) collective-permute-start(bf16[128,512]{1,0:T(8,128)(2,1)S(1)} %get-tuple-element.32), channel_id=1, source_target_pairs={{0,4},{1,5},{2,6},{3,7},{4,8},{5,9},{6,10},{7,11},{8,12},{9,13},{1... | collective-permute-start | bytes 393224 | tf_op jit(solution)/shard_map/ppermute | solution.py:38
  66.0 12.5 %collective-permute-start.14 = (bf16[128,512]{1,0:T(8,128)(2,1)S(1)}, bf16[128,512]{1,0:T(8,128)(2,1)S(1)}, u32[]{:S(2)}, u32[]{:S(2)}) collective-permute-start(bf16[128,512]{1,0:T(8,128)(2,1)S(1)} %get-tuple-element.33), channel_id=1, source_target_pairs={{0,12},{1,13},{2,14},{3,15},{4,0},{5,1},{6,2},{7,3},{8,4},{9,5},{1... | collective-permute-start | bytes 393224 | tf_op jit(solution)/shard_map/ppermute | solution.py:38
  78.7 13.9 %collective-permute-start.15 = (bf16[256,512]{1,0:T(8,128)(2,1)S(1)}, bf16[256,512]{1,0:T(8,128)(2,1)S(1)}, u32[]{:S(2)}, u32[]{:S(2)}) collective-permute-start(bf16[256,512]{1,0:T(8,128)(2,1)S(1)} %get-tuple-element.54), channel_id=1, source_target_pairs={{0,12},{1,13},{2,14},{3,15},{4,0},{5,1},{6,2},{7,3},{8,4},{9,5},{1... | collective-permute-start | bytes 786440 | tf_op jit(solution)/shard_map/ppermute | solution.py:38
  85.3 11.8 %collective-permute-start.13 = (bf16[256,512]{1,0:T(8,128)(2,1)S(1)}, bf16[256,512]{1,0:T(8,128)(2,1)S(1)}, u32[]{:S(2)}, u32[]{:S(2)}) collective-permute-start(bf16[256,512]{1,0:T(8,128)(2,1)S(1)} %get-tuple-element.53), channel_id=1, source_target_pairs={{0,4},{1,5},{2,6},{3,7},{4,8},{5,9},{6,10},{7,11},{8,12},{9,13},{1... | collective-permute-start | bytes 786440 | tf_op jit(solution)/shard_map/ppermute | solution.py:38
  88.1 10.1 %copy-start.6 = (f32[1,256,512]{2,1,0:T(8,128)S(1)}, f32[1,256,512]{2,1,0:T(8,128)}, u32[]{:S(2)}) copy-start(f32[1,256,512]{2,1,0:T(8,128)} %param.19) | copy-start | bytes 1572868
  88.1 10.1 %copy-start.7 = (f32[1,256,512]{2,1,0:T(8,128)S(1)}, f32[1,256,512]{2,1,0:T(8,128)}, u32[]{:S(2)}) copy-start(f32[1,256,512]{2,1,0:T(8,128)} %param.18) | copy-start | bytes 1572868
  100.3 12.2 %collective-permute-start.1 = (bf16[272,512]{1,0:T(8,128)(2,1)S(1)}, bf16[272,512]{1,0:T(8,128)(2,1)}, u32[]{:S(2)}, u32[]{:S(2)}) collective-permute-start(bf16[272,512]{1,0:T(8,128)(2,1)S(1)} %concatenate.44), channel_id=1, source_target_pairs={{480,0},{496,16},{0,32},{16,48},{32,64},{48,80},{64,96},{80,112},{... | collective-permute-start | bytes 835592 | tf_op jit(solution)/shard_map/cond/branch_1_fun/ppermute | solution.py:161
  143.8 1.6 copy-start
  146.9 7.6 %collective-permute-start.6 = (bf16[192,512]{1,0:T(8,128)(2,1)S(1)}, bf16[192,512]{1,0:T(8,128)(2,1)S(1)}, u32[]{:S(2)}, u32[]{:S(2)}) collective-permute-start(bf16[192,512]{1,0:T(8,128)(2,1)S(1)} %get-tuple-element.28), channel_id=1, source_target_pairs={{0,1},{1,0},{2,3},{3,2},{4,5},{5,4},{6,7},{7,6},{8,9},{9,8},{10,11... | collective-permute-start | bytes 589832 | tf_op jit(solution)/shard_map/ppermute | solution.py:42
Sparse Core Ops, SparseCore 0:
  99.7 44.0 all-gather.1

commit v2 on v1

v2 whole, which is shorter than its diff:
```python
from functools import partial

import jax
import jax.numpy as jnp
from jax import lax
from jax.experimental import pallas as pl
from jax.experimental.pallas import tpu as pltpu
from jax.sharding import PartitionSpec as P

D = 4096
KVH = 4
HD = 128
DOCS = 8
KW = 512
TOK = 192
NZ = 8
ROWS = 256
STEP = 48
CHUNKS = TOK // STEP
HALF = NZ * ROWS
FIRST = (3, 1, 5, 7, 4)
REST = (2, 6, 0)


THETA = 1000000.0
BETA_ONE = 0.9
BETA_TWO = 0.95
STEP_RATE = 0.1
WEIGHT_DECAY = 0.2
EPSILON = 1e-08
NORM_EPSILON = 1e-05
FIRST_CORRECTION = 1.0 - 0.9**10
SECOND_CORRECTION = 1.0 - 0.95**10
SCALE = D ** (-0.5)

PARAMS = pltpu.CompilerParams(vmem_limit_bytes=32 * 1024 * 1024)
LARGE = pltpu.CompilerParams(vmem_limit_bytes=57 * 1024 * 1024)
F32, BF16 = jnp.float32, jnp.bfloat16


def along_z(value, distance):
    route = [(f, ((f // 2 + distance) % NZ) * 2 + f % 2) for f in range(2 * NZ)]
    return lax.ppermute(value, "fsdp", route)


def along_z_by_core(value, distance):
    route = []
    for r in range(lax.axis_size("rep")):
        way = distance if r % 2 == 0 else -distance
        for f in range(2 * NZ):
            route.append((r * 2 * NZ + f, r * 2 * NZ + ((f // 2 + way) % NZ) * 2 + f % 2))
    return lax.ppermute(value, ("rep", "fsdp"), route)


def swap_x(value):
    return lax.ppermute(value, "fsdp", [(f, f ^ 1) for f in range(2 * NZ)])


def whole(n):
    return [pl.BlockSpec(memory_space=pltpu.VMEM)] * n


def shapes(*pairs):
    return tuple(jax.ShapeDtypeStruct(shape, dtype) for shape, dtype in pairs)


def cost(size):
    return pl.CostEstimate(flops=0, bytes_accessed=size, transcendentals=0)


def place_of(z, o, side):
    return pl.ds(pl.multiple_of((2 * lax.rem(z + o, NZ) + side) * ROWS, ROWS), ROWS)


def scale_kernel(place, tokens, gain, cotangent, send_first, scales, held, gains, sems):
    z, x = place[0], place[1]
    copies = [pltpu.make_async_copy(gain, gains, sems.at[0])]
    for n in range(CHUNKS):
        rows = pl.ds(n * STEP, STEP)
        copies.append(pltpu.make_async_copy(tokens.at[rows], held.at[rows], sems.at[n + 1]))
    columns = pl.ds(len(FIRST) * ROWS, KW)
    copies.append(pltpu.make_async_copy(cotangent, send_first.at[:, columns], sems.at[CHUNKS + 1]))
    for copy in copies:
        copy.start()
    copies[0].wait()

    def rows_of(i, carry):
        rows = pl.ds(pl.multiple_of(i * 16, 16), 16)
        values = held[rows, :].astype(F32)
        scale = lax.rsqrt(jnp.mean(values * values, axis=-1, keepdims=True) + NORM_EPSILON)
        scales[rows, :] = jnp.broadcast_to(scale, (16, 128))
        for n, o in enumerate(FIRST):
            columns = place_of(z, o, 1 - x)
            part = held[rows, columns].astype(F32) * scale * gains[:, columns]
            send_first[rows, n * ROWS : (n + 1) * ROWS] = part.astype(BF16)
        return carry

    for n in range(CHUNKS):
        copies[n + 1].wait()
        lax.fori_loop(n * STEP // 16, (n + 1) * STEP // 16, rows_of, 0)
    copies[-1].wait()


def normalise_first(place, tokens, gain, cotangent):
    return pl.pallas_call(
        scale_kernel,
        out_shape=shapes(((TOK, len(FIRST) * ROWS + KW), BF16), ((TOK, 128), F32)),
        in_specs=[pl.BlockSpec(memory_space=pltpu.SMEM)] + [pl.BlockSpec(memory_space=pltpu.HBM)] * 3,
        out_specs=whole(2),
        scratch_shapes=[pltpu.VMEM((TOK, D), BF16), pltpu.VMEM((1, D), F32), pltpu.SemaphoreType.DMA((CHUNKS + 2,))],
        compiler_params=LARGE,
        cost_estimate=cost(1 << 10),
        name="normalise_first",
    )(place, tokens, gain, cotangent)


def norm_kernel(place, weight, tokens, gain, scales, numerator, keep, send_rest, model):
    z, x = place[0], place[1]
    model[...] = (numerator[0] / weight[0]).astype(BF16)

    def rows_of(i, carry):
        rows = pl.ds(pl.multiple_of(i * 16, 16), 16)
        scale = scales[rows, :1]

        def part(o, side):
            columns = place_of(z, o, side)
            return (tokens[rows, columns].astype(F32) * scale * gain[:, columns]).astype(BF16)

        for n, o in enumerate(FIRST + REST):
            keep[rows, n * ROWS : (n + 1) * ROWS] = part(o, x)
        for n, o in enumerate(REST):
            send_rest[rows, n * ROWS : (n + 1) * ROWS] = part(o, 1 - x)
        return carry

    lax.fori_loop(0, TOK // 16, rows_of, 0)


def normalise(place, weight, *operands):
    return pl.pallas_call(
        norm_kernel,
        out_shape=shapes(((TOK, HALF), BF16), ((TOK, len(REST) * ROWS), BF16), ((ROWS, KW), BF16)),
        in_specs=[pl.BlockSpec(memory_space=pltpu.SMEM)] * 2 + whole(4),
        out_specs=whole(3),
        compiler_params=PARAMS,
        cost_estimate=cost(1 << 10),
        name="normalise",
    )(place, weight, *operands)


def rotate_rows(cotangent, cosine, sine):
    parts = []
    for h in range(KVH):
        y = cotangent[:, h * HD : (h + 1) * HD].astype(F32)
        s = y * sine
        turned = jnp.concatenate([-s[:, HD // 2 :], s[:, : HD // 2]], axis=-1)
        parts.append(((y * cosine - turned) * SCALE).astype(BF16))
    return jnp.concatenate(parts, axis=-1)


OVER = (((0,), (0,)), ((), ()))


def grad_block(keep, recv, back, n):
    return lax.dot_general(
        keep[:, n * ROWS : (n + 1) * ROWS], back[:TOK], OVER, preferred_element_type=F32
    ) + lax.dot_general(recv[:, n * ROWS : (n + 1) * ROWS], back[TOK:], OVER, preferred_element_type=F32)


def first_kernel(keep, recv, cotangent, cosine, sine, three, one, five, seven, four, back):
    back[:TOK] = rotate_rows(cotangent[...], cosine[:TOK], sine[:TOK])
    back[TOK:] = rotate_rows(recv[:, len(FIRST) * ROWS :], cosine[TOK:], sine[TOK:])
    for n, target in enumerate((three, one, five, seven, four)):
        target[...] = grad_block(keep, recv, back, n).astype(BF16)


def first_parts(keep, recv, cotangent, cosine, sine):
    return pl.pallas_call(
        first_kernel,
        out_shape=shapes(*[((ROWS, KW), BF16)] * 5, ((2 * TOK, KW), BF16)),
        in_specs=whole(5),
        out_specs=whole(6),
        compiler_params=PARAMS,
        cost_estimate=cost(1 << 10),
        name="first_parts",
    )(keep, recv, cotangent, cosine, sine)


def rest_parts(keep, recv, back):
    columns = keep[:, len(FIRST) * ROWS :]
    return lax.dot_general(columns, back[:TOK], OVER, preferred_element_type=F32) + lax.dot_general(
        recv, back[TOK:], OVER, preferred_element_type=F32
    )


def turn_kernel(even, own, above, below, four, up, down):
    extra = four[...].astype(F32)
    share = jnp.full((ROWS, KW), even[0], F32) > 0.5
    up[...] = (own[:ROWS] + above[...].astype(F32) + jnp.where(share, extra, 0.0)).astype(BF16)
    down[...] = (own[ROWS : 2 * ROWS] + below[...].astype(F32) + jnp.where(share, 0.0, extra)).astype(BF16)


def turn(even, *operands):
    return pl.pallas_call(
        turn_kernel,
        out_shape=shapes(*[((ROWS, KW), BF16)] * 2),
        in_specs=[pl.BlockSpec(memory_space=pltpu.SMEM)] + whole(4),
        out_specs=whole(2),
        compiler_params=PARAMS,
        cost_estimate=cost(1 << 10),
        name="turn",
    )(even, *operands)


def near_kernel(even, keep, rest, zero, two, six, one, seven, above, below, far, own, other):
    for target, parts in ((above, (one, zero, six)), (below, (seven, zero, two))):
        for n, part in enumerate(parts):
            target[n * ROWS : (n + 1) * ROWS] = part[...]
    share = jnp.full((ROWS, KW), even[0], F32) > 0.5
    far[...] = jnp.where(share, six[...].astype(F32), two[...].astype(F32)).astype(BF16)
    total = jnp.zeros((TOK, KW), F32)
    for n, ref in enumerate((two, six, zero)):
        total += jnp.dot(rest[:, n * ROWS : (n + 1) * ROWS], ref[...], preferred_element_type=F32)
    other[...] = total
    total = jnp.zeros((TOK, KW), F32)
    for n, ref in enumerate((two, six, zero), len(FIRST)):
        total += jnp.dot(keep[:, n * ROWS : (n + 1) * ROWS], ref[...], preferred_element_type=F32)
    own[...] = total


def near_keys(even, *operands):
    return pl.pallas_call(
        near_kernel,
        out_shape=shapes(
            ((3 * ROWS, KW), BF16),
            ((3 * ROWS, KW), BF16),
            ((ROWS, KW), BF16),
            ((TOK, KW), F32),
            ((TOK, KW), F32),
        ),
        in_specs=[pl.BlockSpec(memory_space=pltpu.SMEM)] + whole(7),
        out_specs=whole(5),
        compiler_params=PARAMS,
        cost_estimate=cost(1 << 10),
        name="near_keys",
    )(even, *operands)


def keys_kernel(keep, first, below, above, far, near_own, near_other, own, other):
    model = {1: below[ROWS : 2 * ROWS], 3: below[2 * ROWS :], 7: above[ROWS : 2 * ROWS], 5: above[2 * ROWS :]}
    model[4] = far[...]
    total = near_other[...]
    for n, o in enumerate(FIRST):
        total += jnp.dot(first[:, n * ROWS : (n + 1) * ROWS], model[o], preferred_element_type=F32)
    other[...] = total.astype(BF16)
    total = near_own[...]
    for n, o in enumerate(FIRST):
        total += jnp.dot(keep[:, n * ROWS : (n + 1) * ROWS], model[o], preferred_element_type=F32)
    own[...] = total


def keys_parts(*operands):
    return pl.pallas_call(
        keys_kernel,
        out_shape=shapes(((TOK, KW), F32), ((TOK, KW), BF16)),
        in_specs=whole(7),
        out_specs=whole(2),
        compiler_params=PARAMS,
        cost_estimate=cost(1 << 10),
        name="keys_parts",
    )(*operands)


def finish_kernel(own, other, cosine, sine, keys):
    for h in range(KVH):
        columns = slice(h * HD, (h + 1) * HD)
        pre = (own[:, columns] + other[:, columns].astype(F32)) * SCALE
        turned = jnp.concatenate([-pre[:, HD // 2 :], pre[:, : HD // 2]], axis=-1)
        keys[:, columns] = (pre * cosine[:TOK] + turned * sine[:TOK]).astype(BF16)


def finish_keys(own, other, cosine, sine):
    return pl.pallas_call(
        finish_kernel,
        out_shape=jax.ShapeDtypeStruct((TOK, KW), BF16),
        in_specs=whole(4),
        out_specs=pl.BlockSpec(memory_space=pltpu.VMEM),
        compiler_params=PARAMS,
        cost_estimate=cost(1 << 10),
        name="finish_keys",
    )(own, other, cosine, sine)


def ready_kernel(weight, own, above, below, numerator, first, second, near, shard, moment, square):
    near[...] = own[2 * ROWS :] + above[:ROWS].astype(F32) + below[:ROWS].astype(F32)
    shard[...] = numerator[0] * (0.5 - 0.5 * STEP_RATE * WEIGHT_DECAY / weight[0])
    moment[...] = BETA_ONE * first[0]
    square[...] = BETA_TWO * second[0]


def ready(weight, *operands):
    return pl.pallas_call(
        ready_kernel,
        out_shape=shapes(*[((ROWS, KW), F32)] * 4),
        in_specs=[pl.BlockSpec(memory_space=pltpu.SMEM)] + whole(6),
        out_specs=whole(4),
        compiler_params=PARAMS,
        cost_estimate=cost(1 << 10),
        name="ready",
    )(weight, *operands)


def step(push_weight, near, shard, moment, square, up, down):
    grad = near + up.astype(F32) + down.astype(F32)
    first = moment + (1.0 - BETA_ONE) * grad
    second = square + (1.0 - BETA_TWO) * grad * grad
    root = jnp.sqrt(second * (1.0 / SECOND_CORRECTION)) + EPSILON
    half = shard - first * (0.5 * STEP_RATE / FIRST_CORRECTION) / root
    message = jnp.concatenate([half, jnp.broadcast_to(0.5 * push_weight[:, None], (16, KW))]).astype(BF16)
    return message, half, first[None], second[None]


def mix_kernel(weight, sent, received, numerator_new, weight_new):
    numerator_new[0] = sent[...] + received[:ROWS].astype(F32)
    weight_new[...] = 0.5 * weight[0] + received[ROWS : ROWS + 1, :128].astype(F32)


def mix(weight, sent, received):
    return pl.pallas_call(
        mix_kernel,
        out_shape=shapes(((1, ROWS, KW), F32), ((1, 128), F32)),
        in_specs=[pl.BlockSpec(memory_space=pltpu.SMEM)] + whole(2),
        out_specs=whole(2),
        compiler_params=PARAMS,
        cost_estimate=cost(1 << 10),
        name="mix",
    )(weight, sent, received)


def push_by(distance, message, keys_operands, cosine, sine):
    n = lax.axis_size("rep")
    received = lax.ppermute(message, "rep", [((i - distance) % n, i) for i in range(n)])
    own_keys, other_keys = keys_parts(*keys_operands)
    keys = finish_keys(own_keys, swap_x(other_keys), cosine, sine)
    return received, keys


def local(
    tokens,
    norm_gain,
    doc_ids,
    key_cotangent,
    numerator,
    first_moment,
    second_moment,
    push_weight,
    gossip_step,
):
    f = lax.axis_index("fsdp")
    z, x = f // 2, f % 2
    even = lax.axis_index("rep") % 2 == 0
    place = jnp.stack([z, x]).astype(jnp.int32)

    share = jnp.where(even, 1.0, 0.0).reshape(1).astype(F32)

    send_first, scales = normalise_first(place, tokens, norm_gain, key_cotangent)
    recv_first = swap_x(send_first)
    other_ids = swap_x(lax.optimization_barrier((doc_ids, scales))[0])
    pair_ids = jnp.concatenate([doc_ids[0], other_ids[0]])
    documents = jnp.arange(DOCS, dtype=jnp.int32)[None, :]
    counts = jnp.sum((pair_ids[:, None] == documents).astype(jnp.int32), axis=0, keepdims=True)
    scales, counts = lax.optimization_barrier((scales, counts))
    keep, send_rest, model = normalise(place, push_weight, tokens, norm_gain, scales, numerator)
    behind_one, behind_two = along_z(counts, 1), along_z(counts, 2)
    before = jnp.where(z >= 1, behind_one, 0) + jnp.where(z >= 2, behind_two, 0)
    row = jnp.arange(TOK, dtype=jnp.int32)
    index = jnp.concatenate([x * TOK + row, (1 - x) * TOK + row])
    shift = jnp.where(pair_ids[:, None] == documents, before, 0)
    shift = shift - jnp.where(pair_ids[:, None] > documents, counts, 0)
    positions = index + jnp.sum(shift, axis=1)
    frequency = THETA ** (-(jnp.arange(HD // 2, dtype=jnp.float32) * 2.0 / HD))
    frequency = jnp.concatenate([frequency, frequency])
    angles = positions.astype(jnp.float32)[:, None] * frequency[None, :]
    cosine, sine = jnp.cos(angles), jnp.sin(angles)

    three, one, five, seven, four, back = first_parts(keep, recv_first, key_cotangent, cosine, sine)
    three, five, four = along_z(three, 1), along_z(five, -1), along_z_by_core(four, 2)
    recv_rest = swap_x(send_rest)
    six, two = along_z(model, 2), along_z(model, -2)
    own = rest_parts(keep, recv_rest, back)
    above, below, far, near_own, near_other = near_keys(share, keep, recv_rest, model, two, six, one, seven)
    above, below, far = along_z(above, 1), along_z(below, -1), along_z_by_core(far, 2)

    up, down = turn(share, own, three, five, four)
    up, down = along_z(up, 2), along_z(down, -2)

    near = ready(push_weight, own, above, below, numerator, first_moment, second_moment)
    message, sent, first_new, second_new = step(push_weight, *near, up, down)
    bit_count = lax.axis_size("rep").bit_length() - 1
    branches = [partial(push_by, 1 << exponent) for exponent in range(bit_count)]
    operands = (keep, recv_first, below, above, far, near_own, near_other)
    received, keys = lax.switch(gossip_step[0] % bit_count, branches, message, operands, cosine, sine)
    numerator_new, weight_new = mix(push_weight, sent, received)
    return (keys, numerator_new, first_new, second_new, weight_new[0, :1])


def solution(mesh):
    in_specs = (
        P(("rep", "fsdp"), None),
        P("rep", None),
        P("rep", "fsdp"),
        P(("rep", "fsdp"), None),
        P("rep", "fsdp", None),
        P("rep", "fsdp", None),
        P("rep", "fsdp", None),
        P("rep"),
        P(),
    )
    out_specs = (
        P(("rep", "fsdp"), None),
        P("rep", "fsdp", None),
        P("rep", "fsdp", None),
        P("rep", "fsdp", None),
        P("rep"),
    )
    return jax.shard_map(local, mesh=mesh, in_specs=in_specs, out_specs=out_specs, check_vma=False)
```

time: 165 us -> 114 us (0.69)
  the two profiles are of different devices: /device:TPU:2 before, /device:TPU:24 now
where the time goes in v2:
time: 114 us; the launch traced here: 113 us
  starting transfers between devices  66.3 us (58%)
  waiting for transfers between devices  21 us (18%)
  Pallas kernels  15.8 us (14%)
  other arithmetic  4.33 us (4%)
  between operations  2.51 us (2%)
  local copies, waits for them, and re-layouts  2.04 us (2%)
    ppermute x10, starting transfers between devices, along_z(): return lax.ppermute(value, 'fsdp', route)  40.7 us
    ppermute x10, waiting for transfers between devices, along_z(): return lax.ppermute(value, 'fsdp', route)  15.9 us
    ppermute x4, starting transfers between devices, swap_x(): return lax.ppermute(value, 'fsdp', [(f, f ^ 1) for f in range(2 * NZ)])  11.7 us
    ppermute x2, starting transfers between devices, along_z_by_core(): return lax.ppermute(value, ('rep', 'fsdp'), route)  9.14 us
    ppermute x4, waiting for transfers between devices, swap_x(): return lax.ppermute(value, 'fsdp', [(f, f ^ 1) for f in range(2 * NZ)])  5.12 us
    ppermute x1, starting transfers between devices, push_by(): lax.ppermute(message, 'rep', [((i - distance) % n, i) for i in range(n)])  4.7 us
    pallas_call x1, Pallas kernels, normalise_first(): pl.pallas_call(scale_kernel, out_shape=shapes(((TOK, len(FIRST) * ROWS +...  4.26 us
    another operation x1, other arithmetic  2.53 us
  transfers between devices with their start and end apart: 17, of which 5 were waited for; matrix products, arithmetic and copies ran while one was open for 4% of the time, Pallas kernels for 9%

profile of v2, /device:TPU:24, one launch (start us, length us, event | category | flops | bytes accessed | tf_op | source)
XLA Modules:
  0.0 112.8 jit_solution(1103056735350631512)
XLA Ops:
  0.6 0.0 copy-start
  0.6 0.0 copy-start.7
  0.7 0.6 pad_add_fusion.1.place
  1.3 4.3 %normalise_first.1 = (bf16[192,1792]{1,0:T(8,128)(2,1)}, f32[192,128]{1,0:T(8,128)}) custom-call(s32[2]{0:T(128)} %pad_add_fusion.1.place, bf16[192,4096]{1,0:T(8,128)(2,1)} %tokens.3, f32[1,4096]{1,0:T(1,128)} %gain.3, bf16[192,512]{1,0:T(8,128)(2,1)} %cotangent.3), custom_call_target="tpu_custom_call" | custom-call | bytes 1024 | tf_op jit(solution)/shard_map/normalise_first/pallas_call | solution.py:105
  5.6 3.4 %collective-permute-start.10 = (s32[1,192]{1,0:T(1,128)S(1)}, s32[1,192]{1,0:T(1,128)S(1)}, u32[]{:S(2)}, u32[]{:S(2)}) collective-permute-start(s32[1,192]{1,0:T(1,128)S(1)} %copy-done.20), channel_id=1, source_target_pairs={{0,1},{1,0},{2,3},{3,2},{4,5},{5,4},{6,7},{7,6},{8,9},{9,8},{10,11... | collective-permute-start | bytes 2312 | tf_op jit(solution)/shard_map/ppermute | solution.py:56
  9.0 2.4 %collective-permute-start.11 = (bf16[192,1792]{1,0:T(8,128)(2,1)}, bf16[192,1792]{1,0:T(8,128)(2,1)S(1)}, u32[]{:S(2)}, u32[]{:S(2)}) collective-permute-start(bf16[192,1792]{1,0:T(8,128)(2,1)} %get-tuple-element.198), channel_id=1, source_target_pairs={{0,1},{1,0},{2,3},{3,2},{4,5},{5,4},{6,7},{7,6},{8,9},{9,8},{10,11... | collective-permute-start | bytes 2064392 | tf_op jit(solution)/shard_map/ppermute | solution.py:56
  11.4 0.1 pad_maximum_fusion
  12.2 0.1 pad_add_fusion
  12.3 0.1 convert_reduce_fusion
  12.4 4.3 %collective-permute-start.12 = (s32[1,8]{1,0:T(1,128)S(1)}, s32[1,8]{1,0:T(1,128)S(1)}, u32[]{:S(2)}, u32[]{:S(2)}) collective-permute-start(s32[1,8]{1,0:T(1,128)S(1)} %bitcast.18), channel_id=1, source_target_pairs={{0,2},{1,3},{2,4},{3,5},{4,6},{5,7},{6,8},{7,9},{8,10},{9,11},{10,... | collective-permute-start | bytes 104 | tf_op jit(solution)/shard_map/ppermute | solution.py:43
  16.7 6.1 %collective-permute-start.13 = (s32[1,8]{1,0:T(1,128)S(1)}, s32[1,8]{1,0:T(1,128)S(1)}, u32[]{:S(2)}, u32[]{:S(2)}) collective-permute-start(s32[1,8]{1,0:T(1,128)S(1)} %bitcast.19), channel_id=1, source_target_pairs={{0,4},{1,5},{2,6},{3,7},{4,8},{5,9},{6,10},{7,11},{8,12},{9,13},{1... | collective-permute-start | bytes 104 | tf_op jit(solution)/shard_map/ppermute | solution.py:43
  22.8 1.0 copy-done.1
  23.9 0.9 copy-done.6
  24.7 1.6 %normalise.1 = (bf16[192,2048]{1,0:T(8,128)(2,1)S(1)}, bf16[192,768]{1,0:T(8,128)(2,1)S(1)}, bf16[256,512]{1,0:T(8,128)(2,1)S(1)}) custom-call(s32[2]{0:T(128)S(1)} %copy-done.8, f32[1]{0:T(128)S(6)} %copy.24.weight, bf16[192,4096]{1,0:T(8,128)(2,1)S(1)} %copy-done, f32[1,4096]{1,0:T(1,128)S(1)} %copy-done.7, f32[192,128]{1,0:T(8,128)S(1)} %copy-done.6, ...), custom_call_target="tpu_custom_call" | custom-call | bytes 1024 | tf_op jit(solution)/shard_map/normalise/pallas_call | solution.py:139
  26.4 5.9 %collective-permute-start.15 = (bf16[256,512]{1,0:T(8,128)(2,1)S(1)}, bf16[256,512]{1,0:T(8,128)(2,1)S(1)}, u32[]{:S(2)}, u32[]{:S(2)}) collective-permute-start(bf16[256,512]{1,0:T(8,128)(2,1)S(1)} %get-tuple-element.202.zero), channel_id=1, source_target_pairs={{0,12},{1,13},{2,14},{3,15},{4,0},{5,1},{6,2},{7,3},{8,4},{9,5},{1... | collective-permute-start | bytes 786440 | tf_op jit(solution)/shard_map/ppermute | solution.py:43
  32.3 2.5 %collective-permute-start.16 = (bf16[256,512]{1,0:T(8,128)(2,1)S(1)}, bf16[256,512]{1,0:T(8,128)(2,1)S(1)}, u32[]{:S(2)}, u32[]{:S(2)}) collective-permute-start(bf16[256,512]{1,0:T(8,128)(2,1)S(1)} %get-tuple-element.202.zero), channel_id=1, source_target_pairs={{0,4},{1,5},{2,6},{3,7},{4,8},{5,9},{6,10},{7,11},{8,12},{9,13},{1... | collective-permute-start | bytes 786440 | tf_op jit(solution)/shard_map/ppermute | solution.py:43
  34.7 3.4 %collective-permute-start.14 = (bf16[192,768]{1,0:T(8,128)(2,1)S(1)}, bf16[192,768]{1,0:T(8,128)(2,1)S(1)}, u32[]{:S(2)}, u32[]{:S(2)}) collective-permute-start(bf16[192,768]{1,0:T(8,128)(2,1)S(1)} %get-tuple-element.201), channel_id=1, source_target_pairs={{0,1},{1,0},{2,3},{3,2},{4,5},{5,4},{6,7},{7,6},{8,9},{9,8},{10,11... | collective-permute-start | bytes 884744 | tf_op jit(solution)/shard_map/ppermute | solution.py:56
  38.2 0.1 subtract_reduce_fusion
  38.3 0.1 fusion.5
  38.3 0.8 multiply_sine_fusion
  39.1 0.0 copy-start.17
  39.2 1.3 %first_parts.1 = (bf16[256,512]{1,0:T(8,128)(2,1)S(1)}, bf16[256,512]{1,0:T(8,128)(2,1)S(1)}, bf16[256,512]{1,0:T(8,128)(2,1)S(1)}, bf16[256,512]{1,0:T(8,128)(2...) custom-call(bf16[192,2048]{1,0:T(8,128)(2,1)S(1)} %get-tuple-element.197.keep, ...), custom_call_target="tpu_custom_call" | custom-call | bytes 1024 | tf_op jit(solution)/shard_map/first_parts/pallas_call | solution.py:177
  40.5 3.9 %collective-permute-start.19 = (bf16[256,512]{1,0:T(8,128)(2,1)S(1)}, bf16[256,512]{1,0:T(8,128)(2,1)S(1)}, u32[]{:S(2)}, u32[]{:S(2)}) collective-permute-start(bf16[256,512]{1,0:T(8,128)(2,1)S(1)} %get-tuple-element.210), channel_id=1, source_target_pairs={{0,2},{1,3},{2,4},{3,5},{4,6},{5,7},{6,8},{7,9},{8,10},{9,11},{10,... | collective-permute-start | bytes 786440 | tf_op jit(solution)/shard_map/ppermute | solution.py:43
  44.4 3.1 %collective-permute-start.20 = (bf16[256,512]{1,0:T(8,128)(2,1)S(1)}, bf16[256,512]{1,0:T(8,128)(2,1)S(1)}, u32[]{:S(2)}, u32[]{:S(2)}) collective-permute-start(bf16[256,512]{1,0:T(8,128)(2,1)S(1)} %get-tuple-element.211), channel_id=1, source_target_pairs={{0,14},{1,15},{2,0},{3,1},{4,2},{5,3},{6,4},{7,5},{8,6},{9,7},{10,... | collective-permute-start | bytes 786440 | tf_op jit(solution)/shard_map/ppermute | solution.py:43
  47.6 4.8 %collective-permute-start.21 = (bf16[256,512]{1,0:T(8,128)(2,1)S(1)}, bf16[256,512]{1,0:T(8,128)(2,1)S(1)}, u32[]{:S(2)}, u32[]{:S(2)}) collective-permute-start(bf16[256,512]{1,0:T(8,128)(2,1)S(1)} %get-tuple-element.212), channel_id=1, source_target_pairs={{0,4},{1,5},{2,6},{3,7},{4,8},{5,9},{6,10},{7,11},{8,12},{9,13},{1... | collective-permute-start | bytes 786440 | tf_op jit(solution)/shard_map/ppermute | solution.py:52
  52.4 1.9 %near_keys.1 = (bf16[768,512]{1,0:T(8,128)(2,1)}, bf16[768,512]{1,0:T(8,128)(2,1)}, bf16[256,512]{1,0:T(8,128)(2,1)S(1)}, f32[192,512]{1,0:T(8,128)}, f32[192,512]{1,0:T(8,128)}) custom-call(f32[1]{0:T(128)} %bitcast.8.even, bf16[192,2048]{1,0:T(8,128)(2,1)S(1)} %get-tuple-element.197.keep, bf16[192,768]{1,0:T(8,128)(2,1)S(1)} %collective-permute-done.14.rest, ...), custom_call_target="tpu_custom_call" | custom-call | bytes 1024 | tf_op jit(solution)/shard_map/near_keys/pallas_call | solution.py:231
  54.3 3.4 %collective-permute-start.17 = (bf16[768,512]{1,0:T(8,128)(2,1)}, bf16[768,512]{1,0:T(8,128)(2,1)}, u32[]{:S(2)}, u32[]{:S(2)}) collective-permute-start(bf16[768,512]{1,0:T(8,128)(2,1)} %get-tuple-element.205), channel_id=1, source_target_pairs={{0,2},{1,3},{2,4},{3,5},{4,6},{5,7},{6,8},{7,9},{8,10},{9,11},{10,... | collective-permute-start | bytes 2359304 | tf_op jit(solution)/shard_map/ppermute | solution.py:43
  57.7 3.7 %collective-permute-start.18 = (bf16[768,512]{1,0:T(8,128)(2,1)}, bf16[768,512]{1,0:T(8,128)(2,1)}, u32[]{:S(2)}, u32[]{:S(2)}) collective-permute-start(bf16[768,512]{1,0:T(8,128)(2,1)} %get-tuple-element.206), channel_id=1, source_target_pairs={{0,14},{1,15},{2,0},{3,1},{4,2},{5,3},{6,4},{7,5},{8,6},{9,7},{10,... | collective-permute-start | bytes 2359304 | tf_op jit(solution)/shard_map/ppermute | solution.py:43
  61.3 0.4 fusion.2
  61.8 0.4 convolution_add_fusion.own
  62.2 0.0 copy-start.2
  62.2 0.9 turn.1
  63.2 4.8 %collective-permute-start.22 = (bf16[256,512]{1,0:T(8,128)(2,1)}, bf16[256,512]{1,0:T(8,128)(2,1)}, u32[]{:S(2)}, u32[]{:S(2)}) collective-permute-start(bf16[256,512]{1,0:T(8,128)(2,1)} %get-tuple-element.213), channel_id=1, source_target_pairs={{0,4},{1,5},{2,6},{3,7},{4,8},{5,9},{6,10},{7,11},{8,12},{9,13},{1... | collective-permute-start | bytes 786440 | tf_op jit(solution)/shard_map/ppermute | solution.py:43
  68.0 3.1 %collective-permute-start.23 = (bf16[256,512]{1,0:T(8,128)(2,1)}, bf16[256,512]{1,0:T(8,128)(2,1)}, u32[]{:S(2)}, u32[]{:S(2)}) collective-permute-start(bf16[256,512]{1,0:T(8,128)(2,1)} %get-tuple-element.214), channel_id=1, source_target_pairs={{0,12},{1,13},{2,14},{3,15},{4,0},{5,1},{6,2},{7,3},{8,4},{9,5},{1... | collective-permute-start | bytes 786440 | tf_op jit(solution)/shard_map/ppermute | solution.py:43
  71.8 4.3 %collective-permute-start.24 = (bf16[256,512]{1,0:T(8,128)(2,1)S(1)}, bf16[256,512]{1,0:T(8,128)(2,1)S(1)}, u32[]{:S(2)}, u32[]{:S(2)}) collective-permute-start(bf16[256,512]{1,0:T(8,128)(2,1)S(1)} %get-tuple-element.216), channel_id=1, source_target_pairs={{0,4},{1,5},{2,6},{3,7},{4,8},{5,9},{6,10},{7,11},{8,12},{9,13},{1... | collective-permute-start | bytes 786440 | tf_op jit(solution)/shard_map/ppermute | solution.py:52
  76.1 7.1 %collective-permute-done.17.above = bf16[768,512]{1,0:T(8,128)(2,1)} collective-permute-done((bf16[768,512]{1,0:T(8,128)(2,1)}, bf16[768,512]{1,0:T(8,128)(2,1)}, u32[]{:S(2)}, u32[]{:S(2)}) %collective-permute-start.17) | collective-permute-done | bytes 786464 | tf_op jit(solution)/shard_map/ppermute | solution.py:43
  83.2 1.9 %collective-permute-done.18.below = bf16[768,512]{1,0:T(8,128)(2,1)} collective-permute-done((bf16[768,512]{1,0:T(8,128)(2,1)}, bf16[768,512]{1,0:T(8,128)(2,1)}, u32[]{:S(2)}, u32[]{:S(2)}) %collective-permute-start.18) | collective-permute-done | bytes 786464 | tf_op jit(solution)/shard_map/ppermute | solution.py:43
  85.1 1.6 %ready.1 = (f32[256,512]{1,0:T(8,128)S(1)}, f32[256,512]{1,0:T(8,128)S(1)}, f32[256,512]{1,0:T(8,128)S(1)}, f32[256,512]{1,0:T(8,128)S(1)}) custom-call(f32[1]{0:T(128)S(6)} %copy.24.weight, f32[768,512]{1,0:T(8,128)S(1)} %convolution_add_fusion.own, bf16[768,512]{1,0:T(8,128)(2,1)} %collective-permute-done.17.above, ...), custom_call_target="tpu_custom_call" | custom-call | bytes 1024 | tf_op jit(solution)/shard_map/ready/pallas_call | solution.py:301
  86.8 1.1 collective-permute-done.22
  87.9 5.8 %collective-permute-done.23 = bf16[256,512]{1,0:T(8,128)(2,1)} collective-permute-done((bf16[256,512]{1,0:T(8,128)(2,1)}, bf16[256,512]{1,0:T(8,128)(2,1)}, u32[]{:S(2)}, u32[]{:S(2)}) %collective-permute-start.23) | collective-permute-done | bytes 262176 | tf_op jit(solution)/shard_map/ppermute | solution.py:43
  93.7 2.5 %fusion.10 = (bf16[256,512]{1,0:T(8,128)(2,1)S(1)}, f32[256,512]{1,0:T(8,128)S(1)}, f32[1,256,512]{2,1,0:T(8,128)}, f32[1,256,512]{2,1,0:T(8,128)}) fusion(f32[256,512]{1,0:T(8,128)S(1)} %get-tuple-element.207, f32[256,512]{1,0:T(8,128)S(1)} %get-tuple-element.215, f32[256,512]{1,0:T(8,128)S(1)} %get-tuple-element.208, ...), kind=kLoop, calls=%fused_computation.30 | loop fusion | flops 1966080 | bytes 4456448 | tf_op jit(solution)/shard_map/convert
  96.3 14.7 %conditional.1 = (bf16[272,512]{1,0:T(8,128)(2,1)}, bf16[192,512]{1,0:T(8,128)(2,1)S(1)}) conditional(s32[]{:T(128)} %clamp.3, (bf16[272,512]{1,0:T(8,128)(2,1)S(1)}, bf16[192,2048]{1,0:T(8,128)(2,1)S(1)}, bf16[192,1792]{1,0:T(8,128)(2,1)S(1)}, bf16[768,512]{1,0:T(8,128)(2,1)}, bf16[768,512]{1,0:T(8,128)(2,1)}, ...), branch_computations={%region_2.3_spmd, %region_3.4_spmd, %region_4.5_spmd, %region_5.6_... | conditional | bytes 1902688 | solution.py:401
  96.3 4.7 %collective-permute-start.2 = (bf16[272,512]{1,0:T(8,128)(2,1)S(1)}, bf16[272,512]{1,0:T(8,128)(2,1)}, u32[]{:S(2)}, u32[]{:S(2)}) collective-permute-start(bf16[272,512]{1,0:T(8,128)(2,1)S(1)} %get-tuple-element.112), channel_id=1, source_target_pairs={{480,0},{496,16},{0,32},{16,48},{32,64},{48,80},{64,96},{80,112},{... | collective-permute-start | bytes 835592 | tf_op jit(solution)/shard_map/cond/branch_1_fun/ppermute | solution.py:341
  101.0 2.0 %keys_parts.6 = (f32[192,512]{1,0:T(8,128)S(1)}, bf16[192,512]{1,0:T(8,128)(2,1)S(1)}) custom-call(bf16[192,2048]{1,0:T(8,128)(2,1)S(1)} %get-tuple-element.113.keep, bf16[192,1792]{1,0:T(8,128)(2,1)S(1)} %get-tuple-element.114.first, bf16[768,512]{1,0:T(8,128)(2,1)} %get-tuple-element.115.below, bf16[768,512]{1,0:T(8,128)(2,1)} %get-tuple-element.116.above, ...), custom_call_target="tpu_custom_call" | custom-call | bytes 1024 | tf_op jit(solution)/shard_map/cond/branch_1_fun/keys_parts/pallas_call | solution.py:262
  103.1 2.4 %collective-permute-start.3 = (bf16[192,512]{1,0:T(8,128)(2,1)S(1)}, bf16[192,512]{1,0:T(8,128)(2,1)S(1)}, u32[]{:S(2)}, u32[]{:S(2)}) collective-permute-start(bf16[192,512]{1,0:T(8,128)(2,1)S(1)} %get-tuple-element.121), channel_id=1, source_target_pairs={{0,1},{1,0},{2,3},{3,2},{4,5},{5,4},{6,7},{7,6},{8,9},{9,8},{10,11... | collective-permute-start | bytes 589832 | tf_op jit(solution)/shard_map/cond/branch_1_fun/ppermute | solution.py:56
  105.5 5.1 %collective-permute-done.3.other = bf16[192,512]{1,0:T(8,128)(2,1)S(1)} collective-permute-done((bf16[192,512]{1,0:T(8,128)(2,1)S(1)}, bf16[192,512]{1,0:T(8,128)(2,1)S(1)}, u32[]{:S(2)}, u32[]{:S(2)}) %collective-permute-start.3) | collective-permute-done | bytes 196640 | tf_op jit(solution)/shard_map/cond/branch_1_fun/ppermute | solution.py:56
  110.7 0.3 finish_keys.6
  111.0 1.9 %mix.1 = (f32[1,256,512]{2,1,0:T(8,128)}, f32[1,128]{1,0:T(1,128)}) custom-call(f32[1]{0:T(128)S(6)} %copy.24.weight, f32[256,512]{1,0:T(8,128)S(1)} %get-tuple-element.224.sent, bf16[272,512]{1,0:T(8,128)(2,1)} %get-tuple-element.220.received), custom_call_target="tpu_custom_call" | custom-call | bytes 1024 | tf_op jit(solution)/shard_map/mix/pallas_call | solution.py:328
  (52 shorter events, 0.2 us)
Async XLA Ops:
  0.6 22.1 %copy-start = (bf16[192,4096]{1,0:T(8,128)(2,1)S(1)}, bf16[192,4096]{1,0:T(8,128)(2,1)}, u32[]{:S(2)}) copy-start(bf16[192,4096]{1,0:T(8,128)(2,1)} %tokens.3) | copy-start | bytes 4718596
  0.6 22.1 %copy-start.7 = (f32[1,4096]{1,0:T(1,128)S(1)}, f32[1,4096]{1,0:T(1,128)}, u32[]{:S(2)}) copy-start(f32[1,4096]{1,0:T(1,128)} %gain.3) | copy-start | bytes 49156
  0.7 4.9 %copy-start.20 = (s32[1,192]{1,0:T(1,128)S(1)}, s32[1,192]{1,0:T(1,128)}, u32[]{:S(2)}) copy-start(s32[1,192]{1,0:T(1,128)} %param.16) | copy-start | bytes 2308
  1.3 21.5 %copy-start.8 = (s32[2]{0:T(128)S(1)}, s32[2]{0:T(128)}, u32[]{:S(2)}) copy-start(s32[2]{0:T(128)} %pad_add_fusion.1.place) | copy-start | bytes 28
  1.3 37.9 %copy-start.3 = (bf16[192,512]{1,0:T(8,128)(2,1)S(1)}, bf16[192,512]{1,0:T(8,128)(2,1)}, u32[]{:S(2)}) copy-start(bf16[192,512]{1,0:T(8,128)(2,1)} %cotangent.3) | copy-start | bytes 589828
  5.6 6.6 %collective-permute-start.10 = (s32[1,192]{1,0:T(1,128)S(1)}, s32[1,192]{1,0:T(1,128)S(1)}, u32[]{:S(2)}, u32[]{:S(2)}) collective-permute-start(s32[1,192]{1,0:T(1,128)S(1)} %copy-done.20), channel_id=1, source_target_pairs={{0,1},{1,0},{2,3},{3,2},{4,5},{5,4},{6,7},{7,6},{8,9},{9,8},{10,11... | collective-permute-start | bytes 2312 | tf_op jit(solution)/shard_map/ppermute | solution.py:56
  9.0 30.2 %collective-permute-start.11 = (bf16[192,1792]{1,0:T(8,128)(2,1)}, bf16[192,1792]{1,0:T(8,128)(2,1)S(1)}, u32[]{:S(2)}, u32[]{:S(2)}) collective-permute-start(bf16[192,1792]{1,0:T(8,128)(2,1)} %get-tuple-element.198), channel_id=1, source_target_pairs={{0,1},{1,0},{2,3},{3,2},{4,5},{5,4},{6,7},{7,6},{8,9},{9,8},{10,11... | collective-permute-start | bytes 2064392 | tf_op jit(solution)/shard_map/ppermute | solution.py:56
  12.4 22.3 %collective-permute-start.12 = (s32[1,8]{1,0:T(1,128)S(1)}, s32[1,8]{1,0:T(1,128)S(1)}, u32[]{:S(2)}, u32[]{:S(2)}) collective-permute-start(s32[1,8]{1,0:T(1,128)S(1)} %bitcast.18), channel_id=1, source_target_pairs={{0,2},{1,3},{2,4},{3,5},{4,6},{5,7},{6,8},{7,9},{8,10},{9,11},{10,... | collective-permute-start | bytes 104 | tf_op jit(solution)/shard_map/ppermute | solution.py:43
  16.7 21.5 %collective-permute-start.13 = (s32[1,8]{1,0:T(1,128)S(1)}, s32[1,8]{1,0:T(1,128)S(1)}, u32[]{:S(2)}, u32[]{:S(2)}) collective-permute-start(s32[1,8]{1,0:T(1,128)S(1)} %bitcast.19), channel_id=1, source_target_pairs={{0,4},{1,5},{2,6},{3,7},{4,8},{5,9},{6,10},{7,11},{8,12},{9,13},{1... | collective-permute-start | bytes 104 | tf_op jit(solution)/shard_map/ppermute | solution.py:43
  22.8 1.0 copy-start.1
  23.9 0.9 copy-start.6
  26.4 35.4 %copy-start.9 = (bf16[192,2048]{1,0:T(8,128)(2,1)}, bf16[192,2048]{1,0:T(8,128)(2,1)S(1)}, u32[]{:S(2)}) copy-start(bf16[192,2048]{1,0:T(8,128)(2,1)S(1)} %get-tuple-element.197.keep) | copy-start | bytes 2359300
  26.4 21.2 %collective-permute-start.15 = (bf16[256,512]{1,0:T(8,128)(2,1)S(1)}, bf16[256,512]{1,0:T(8,128)(2,1)S(1)}, u32[]{:S(2)}, u32[]{:S(2)}) collective-permute-start(bf16[256,512]{1,0:T(8,128)(2,1)S(1)} %get-tuple-element.202.zero), channel_id=1, source_target_pairs={{0,12},{1,13},{2,14},{3,15},{4,0},{5,1},{6,2},{7,3},{8,4},{9,5},{1... | collective-permute-start | bytes 786440 | tf_op jit(solution)/shard_map/ppermute | solution.py:43
  32.3 20.1 %collective-permute-start.16 = (bf16[256,512]{1,0:T(8,128)(2,1)S(1)}, bf16[256,512]{1,0:T(8,128)(2,1)S(1)}, u32[]{:S(2)}, u32[]{:S(2)}) collective-permute-start(bf16[256,512]{1,0:T(8,128)(2,1)S(1)} %get-tuple-element.202.zero), channel_id=1, source_target_pairs={{0,4},{1,5},{2,6},{3,7},{4,8},{5,9},{6,10},{7,11},{8,12},{9,13},{1... | collective-permute-start | bytes 786440 | tf_op jit(solution)/shard_map/ppermute | solution.py:43
  34.7 17.7 %collective-permute-start.14 = (bf16[192,768]{1,0:T(8,128)(2,1)S(1)}, bf16[192,768]{1,0:T(8,128)(2,1)S(1)}, u32[]{:S(2)}, u32[]{:S(2)}) collective-permute-start(bf16[192,768]{1,0:T(8,128)(2,1)S(1)} %get-tuple-element.201), channel_id=1, source_target_pairs={{0,1},{1,0},{2,3},{3,2},{4,5},{5,4},{6,7},{7,6},{8,9},{9,8},{10,11... | collective-permute-start | bytes 884744 | tf_op jit(solution)/shard_map/ppermute | solution.py:56
  39.1 1.4 %copy-start.15 = (f32[384,128]{1,0:T(8,128)}, f32[384,128]{1,0:T(8,128)S(1)}, u32[]{:S(2)}) copy-start(f32[384,128]{1,0:T(8,128)S(1)} %get-tuple-element.227.sine) | copy-start | bytes 589828
  39.1 15.2 %copy-start.17 = (f32[384,128]{1,0:T(8,128)}, f32[384,128]{1,0:T(8,128)S(1)}, u32[]{:S(2)}) copy-start(f32[384,128]{1,0:T(8,128)S(1)} %get-tuple-element.228.cosine) | copy-start | bytes 589828
  39.1 13.3 %copy-start.11 = (bf16[192,1792]{1,0:T(8,128)(2,1)}, bf16[192,1792]{1,0:T(8,128)(2,1)S(1)}, u32[]{:S(2)}) copy-start(bf16[192,1792]{1,0:T(8,128)(2,1)S(1)} %collective-permute-done.11.recv) | copy-start | bytes 2064388
  40.5 21.7 %collective-permute-start.19 = (bf16[256,512]{1,0:T(8,128)(2,1)S(1)}, bf16[256,512]{1,0:T(8,128)(2,1)S(1)}, u32[]{:S(2)}, u32[]{:S(2)}) collective-permute-start(bf16[256,512]{1,0:T(8,128)(2,1)S(1)} %get-tuple-element.210), channel_id=1, source_target_pairs={{0,2},{1,3},{2,4},{3,5},{4,6},{5,7},{6,8},{7,9},{8,10},{9,11},{10,... | collective-permute-start | bytes 786440 | tf_op jit(solution)/shard_map/ppermute | solution.py:43
  44.4 17.8 %collective-permute-start.20 = (bf16[256,512]{1,0:T(8,128)(2,1)S(1)}, bf16[256,512]{1,0:T(8,128)(2,1)S(1)}, u32[]{:S(2)}, u32[]{:S(2)}) collective-permute-start(bf16[256,512]{1,0:T(8,128)(2,1)S(1)} %get-tuple-element.211), channel_id=1, source_target_pairs={{0,14},{1,15},{2,0},{3,1},{4,2},{5,3},{6,4},{7,5},{8,6},{9,7},{10,... | collective-permute-start | bytes 786440 | tf_op jit(solution)/shard_map/ppermute | solution.py:43
  47.6 14.7 %collective-permute-start.21 = (bf16[256,512]{1,0:T(8,128)(2,1)S(1)}, bf16[256,512]{1,0:T(8,128)(2,1)S(1)}, u32[]{:S(2)}, u32[]{:S(2)}) collective-permute-start(bf16[256,512]{1,0:T(8,128)(2,1)S(1)} %get-tuple-element.212), channel_id=1, source_target_pairs={{0,4},{1,5},{2,6},{3,7},{4,8},{5,9},{6,10},{7,11},{8,12},{9,13},{1... | collective-permute-start | bytes 786440 | tf_op jit(solution)/shard_map/ppermute | solution.py:52
  54.3 29.0 %collective-permute-start.17 = (bf16[768,512]{1,0:T(8,128)(2,1)}, bf16[768,512]{1,0:T(8,128)(2,1)}, u32[]{:S(2)}, u32[]{:S(2)}) collective-permute-start(bf16[768,512]{1,0:T(8,128)(2,1)} %get-tuple-element.205), channel_id=1, source_target_pairs={{0,2},{1,3},{2,4},{3,5},{4,6},{5,7},{6,8},{7,9},{8,10},{9,11},{10,... | collective-permute-start | bytes 2359304 | tf_op jit(solution)/shard_map/ppermute | solution.py:43
  57.7 27.5 %collective-permute-start.18 = (bf16[768,512]{1,0:T(8,128)(2,1)}, bf16[768,512]{1,0:T(8,128)(2,1)}, u32[]{:S(2)}, u32[]{:S(2)}) collective-permute-start(bf16[768,512]{1,0:T(8,128)(2,1)} %get-tuple-element.206), channel_id=1, source_target_pairs={{0,14},{1,15},{2,0},{3,1},{4,2},{5,3},{6,4},{7,5},{8,6},{9,7},{10,... | collective-permute-start | bytes 2359304 | tf_op jit(solution)/shard_map/ppermute | solution.py:43
  62.2 23.0 %copy-start.2 = (f32[1,256,512]{2,1,0:T(8,128)S(1)}, f32[1,256,512]{2,1,0:T(8,128)}, u32[]{:S(2)}) copy-start(f32[1,256,512]{2,1,0:T(8,128)} %numerator.3) | copy-start | bytes 1572868
  62.2 23.0 %copy-start.4 = (f32[1,256,512]{2,1,0:T(8,128)S(1)}, f32[1,256,512]{2,1,0:T(8,128)}, u32[]{:S(2)}) copy-start(f32[1,256,512]{2,1,0:T(8,128)} %first.1) | copy-start | bytes 1572868
  62.2 22.9 %copy-start.5 = (f32[1,256,512]{2,1,0:T(8,128)S(1)}, f32[1,256,512]{2,1,0:T(8,128)}, u32[]{:S(2)}) copy-start(f32[1,256,512]{2,1,0:T(8,128)} %second.1) | copy-start | bytes 1572868
  63.2 24.7 %collective-permute-start.22 = (bf16[256,512]{1,0:T(8,128)(2,1)}, bf16[256,512]{1,0:T(8,128)(2,1)}, u32[]{:S(2)}, u32[]{:S(2)}) collective-permute-start(bf16[256,512]{1,0:T(8,128)(2,1)} %get-tuple-element.213), channel_id=1, source_target_pairs={{0,4},{1,5},{2,6},{3,7},{4,8},{5,9},{6,10},{7,11},{8,12},{9,13},{1... | collective-permute-start | bytes 786440 | tf_op jit(solution)/shard_map/ppermute | solution.py:43
  68.0 25.7 %collective-permute-start.23 = (bf16[256,512]{1,0:T(8,128)(2,1)}, bf16[256,512]{1,0:T(8,128)(2,1)}, u32[]{:S(2)}, u32[]{:S(2)}) collective-permute-start(bf16[256,512]{1,0:T(8,128)(2,1)} %get-tuple-element.214), channel_id=1, source_target_pairs={{0,12},{1,13},{2,14},{3,15},{4,0},{5,1},{6,2},{7,3},{8,4},{9,5},{1... | collective-permute-start | bytes 786440 | tf_op jit(solution)/shard_map/ppermute | solution.py:43
  71.8 24.4 %collective-permute-start.24 = (bf16[256,512]{1,0:T(8,128)(2,1)S(1)}, bf16[256,512]{1,0:T(8,128)(2,1)S(1)}, u32[]{:S(2)}, u32[]{:S(2)}) collective-permute-start(bf16[256,512]{1,0:T(8,128)(2,1)S(1)} %get-tuple-element.216), channel_id=1, source_target_pairs={{0,4},{1,5},{2,6},{3,7},{4,8},{5,9},{6,10},{7,11},{8,12},{9,13},{1... | collective-permute-start | bytes 786440 | tf_op jit(solution)/shard_map/ppermute | solution.py:52
  93.6 2.6 %copy-start.10 = (bf16[192,2048]{1,0:T(8,128)(2,1)S(1)}, bf16[192,2048]{1,0:T(8,128)(2,1)}, u32[]{:S(2)}) copy-start(bf16[192,2048]{1,0:T(8,128)(2,1)} %copy-done.9) | copy-start | bytes 2359300
  93.6 2.6 %copy-start.12 = (bf16[192,1792]{1,0:T(8,128)(2,1)S(1)}, bf16[192,1792]{1,0:T(8,128)(2,1)}, u32[]{:S(2)}) copy-start(bf16[192,1792]{1,0:T(8,128)(2,1)} %copy-done.11) | copy-start | bytes 2064388
  93.6 2.6 %copy-start.13 = (f32[192,512]{1,0:T(8,128)S(1)}, f32[192,512]{1,0:T(8,128)}, u32[]{:S(2)}) copy-start(f32[192,512]{1,0:T(8,128)} %get-tuple-element.217) | copy-start | bytes 1179652
  93.7 2.6 %copy-start.14 = (f32[192,512]{1,0:T(8,128)S(1)}, f32[192,512]{1,0:T(8,128)}, u32[]{:S(2)}) copy-start(f32[192,512]{1,0:T(8,128)} %get-tuple-element.218) | copy-start | bytes 1179652
  93.7 2.6 %copy-start.16 = (f32[384,128]{1,0:T(8,128)S(1)}, f32[384,128]{1,0:T(8,128)}, u32[]{:S(2)}) copy-start(f32[384,128]{1,0:T(8,128)} %copy-done.15) | copy-start | bytes 589828
  93.7 2.6 %copy-start.18 = (f32[384,128]{1,0:T(8,128)S(1)}, f32[384,128]{1,0:T(8,128)}, u32[]{:S(2)}) copy-start(f32[384,128]{1,0:T(8,128)} %copy-done.17) | copy-start | bytes 589828
  96.3 14.6 %collective-permute-start.2 = (bf16[272,512]{1,0:T(8,128)(2,1)S(1)}, bf16[272,512]{1,0:T(8,128)(2,1)}, u32[]{:S(2)}, u32[]{:S(2)}) collective-permute-start(bf16[272,512]{1,0:T(8,128)(2,1)S(1)} %get-tuple-element.112), channel_id=1, source_target_pairs={{480,0},{496,16},{0,32},{16,48},{32,64},{48,80},{64,96},{80,112},{... | collective-permute-start | bytes 835592 | tf_op jit(solution)/shard_map/cond/branch_1_fun/ppermute | solution.py:341
  103.1 7.6 %collective-permute-start.3 = (bf16[192,512]{1,0:T(8,128)(2,1)S(1)}, bf16[192,512]{1,0:T(8,128)(2,1)S(1)}, u32[]{:S(2)}, u32[]{:S(2)}) collective-permute-start(bf16[192,512]{1,0:T(8,128)(2,1)S(1)} %get-tuple-element.121), channel_id=1, source_target_pairs={{0,1},{1,0},{2,3},{3,2},{4,5},{5,4},{6,7},{7,6},{8,9},{9,8},{10,11... | collective-permute-start | bytes 589832 | tf_op jit(solution)/shard_map/cond/branch_1_fun/ppermute | solution.py:56
  111.0 1.9 %copy-start.19 = (bf16[192,512]{1,0:T(8,128)(2,1)}, bf16[192,512]{1,0:T(8,128)(2,1)S(1)}, u32[]{:S(2)}) copy-start(bf16[192,512]{1,0:T(8,128)(2,1)S(1)} %get-tuple-element.189) | copy-start | bytes 589828

commit v3 on v2

--- a/solution.py
+++ b/solution.py
@@ -72,14 +72,26 @@
     return pl.ds(pl.multiple_of((2 * lax.rem(z + o, NZ) + side) * ROWS, ROWS), ROWS)
 
 
-def scale_kernel(place, tokens, gain, cotangent, send_first, scales, held, gains, sems):
-    z, x = place[0], place[1]
+def place():
+    f = lax.axis_index("fsdp")
+    return lax.div(f, 2), lax.rem(f, 2)
+
+
+def even_core():
+    return lax.rem(lax.axis_index("rep"), 2) == 0
+
+
+def scale_kernel(
+    weight, tokens, gain, cotangent, numerator, send_first, scales, model, held, gains, shard, sems
+):
+    z, x = place()
     copies = [pltpu.make_async_copy(gain, gains, sems.at[0])]
     for n in range(CHUNKS):
         rows = pl.ds(n * STEP, STEP)
         copies.append(pltpu.make_async_copy(tokens.at[rows], held.at[rows], sems.at[n + 1]))
     columns = pl.ds(len(FIRST) * ROWS, KW)
     copies.append(pltpu.make_async_copy(cotangent, send_first.at[:, columns], sems.at[CHUNKS + 1]))
+    copies.append(pltpu.make_async_copy(numerator.at[0], shard, sems.at[CHUNKS + 2]))
     for copy in copies:
         copy.start()
     copies[0].wait()
@@ -98,25 +110,35 @@
     for n in range(CHUNKS):
         copies[n + 1].wait()
         lax.fori_loop(n * STEP // 16, (n + 1) * STEP // 16, rows_of, 0)
+    copies[-2].wait()
     copies[-1].wait()
-
-
-def normalise_first(place, tokens, gain, cotangent):
+    model[...] = (shard[...] / weight[0]).astype(BF16)
+
+
+def normalise_first(weight, *operands):
     return pl.pallas_call(
         scale_kernel,
-        out_shape=shapes(((TOK, len(FIRST) * ROWS + KW), BF16), ((TOK, 128), F32)),
-        in_specs=[pl.BlockSpec(memory_space=pltpu.SMEM)] + [pl.BlockSpec(memory_space=pltpu.HBM)] * 3,
-        out_specs=whole(2),
-        scratch_shapes=[pltpu.VMEM((TOK, D), BF16), pltpu.VMEM((1, D), F32), pltpu.SemaphoreType.DMA((CHUNKS + 2,))],
+        out_shape=shapes(
+            ((TOK, len(FIRST) * ROWS + KW), BF16),
+            ((TOK, 128), F32),
+            ((ROWS, KW), BF16),
+        ),
+        in_specs=[pl.BlockSpec(memory_space=pltpu.SMEM)] + [pl.BlockSpec(memory_space=pltpu.HBM)] * 4,
+        out_specs=whole(3),
+        scratch_shapes=[
+            pltpu.VMEM((TOK, D), BF16),
+            pltpu.VMEM((1, D), F32),
+            pltpu.VMEM((ROWS, KW), F32),
+            pltpu.SemaphoreType.DMA((CHUNKS + 3,)),
+        ],
         compiler_params=LARGE,
         cost_estimate=cost(1 << 10),
         name="normalise_first",
-    )(place, tokens, gain, cotangent)
-
-
-def norm_kernel(place, weight, tokens, gain, scales, numerator, keep, send_rest, model):
-    z, x = place[0], place[1]
-    model[...] = (numerator[0] / weight[0]).astype(BF16)
+    )(weight, *operands)
+
+
+def norm_kernel(tokens, gain, scales, keep, send_rest):
+    z, x = place()
 
     def rows_of(i, carry):
         rows = pl.ds(pl.multiple_of(i * 16, 16), 16)
@@ -135,16 +157,16 @@
     lax.fori_loop(0, TOK // 16, rows_of, 0)
 
 
-def normalise(place, weight, *operands):
+def normalise(*operands):
     return pl.pallas_call(
         norm_kernel,
-        out_shape=shapes(((TOK, HALF), BF16), ((TOK, len(REST) * ROWS), BF16), ((ROWS, KW), BF16)),
-        in_specs=[pl.BlockSpec(memory_space=pltpu.SMEM)] * 2 + whole(4),
-        out_specs=whole(3),
+        out_shape=shapes(((TOK, HALF), BF16), ((TOK, len(REST) * ROWS), BF16)),
+        in_specs=whole(3),
+        out_specs=whole(2),
         compiler_params=PARAMS,
         cost_estimate=cost(1 << 10),
         name="normalise",
-    )(place, weight, *operands)
+    )(*operands)
 
 
 def rotate_rows(cotangent, cosine, sine):
@@ -166,19 +188,19 @@
     ) + lax.dot_general(recv[:, n * ROWS : (n + 1) * ROWS], back[TOK:], OVER, preferred_element_type=F32)
 
 
-def first_kernel(keep, recv, cotangent, cosine, sine, three, one, five, seven, four, back):
+def first_kernel(keep, recv, cotangent, cosine, sine, up, down, four, back):
     back[:TOK] = rotate_rows(cotangent[...], cosine[:TOK], sine[:TOK])
     back[TOK:] = rotate_rows(recv[:, len(FIRST) * ROWS :], cosine[TOK:], sine[TOK:])
-    for n, target in enumerate((three, one, five, seven, four)):
+    for n, target in enumerate((up.at[:ROWS], up.at[ROWS:], down.at[:ROWS], down.at[ROWS:], four)):
         target[...] = grad_block(keep, recv, back, n).astype(BF16)
 
 
 def first_parts(keep, recv, cotangent, cosine, sine):
     return pl.pallas_call(
         first_kernel,
-        out_shape=shapes(*[((ROWS, KW), BF16)] * 5, ((2 * TOK, KW), BF16)),
+        out_shape=shapes(*[((2 * ROWS, KW), BF16)] * 2, ((ROWS, KW), BF16), ((2 * TOK, KW), BF16)),
         in_specs=whole(5),
-        out_specs=whole(6),
+        out_specs=whole(4),
         compiler_params=PARAMS,
         cost_estimate=cost(1 << 10),
         name="first_parts",
@@ -192,68 +214,55 @@
     )
 
 
-def turn_kernel(even, own, above, below, four, up, down):
+def turn_kernel(own, above, below, four, up, down):
     extra = four[...].astype(F32)
-    share = jnp.full((ROWS, KW), even[0], F32) > 0.5
-    up[...] = (own[:ROWS] + above[...].astype(F32) + jnp.where(share, extra, 0.0)).astype(BF16)
-    down[...] = (own[ROWS : 2 * ROWS] + below[...].astype(F32) + jnp.where(share, 0.0, extra)).astype(BF16)
-
-
-def turn(even, *operands):
+    share = jnp.full((ROWS, KW), even_core().astype(F32)) > 0.5
+    up[...] = (own[:ROWS] + above[:ROWS].astype(F32) + jnp.where(share, extra, 0.0)).astype(BF16)
+    down[...] = (own[ROWS : 2 * ROWS] + below[:ROWS].astype(F32) + jnp.where(share, 0.0, extra)).astype(BF16)
+
+
+def turn(*operands):
     return pl.pallas_call(
         turn_kernel,
         out_shape=shapes(*[((ROWS, KW), BF16)] * 2),
-        in_specs=[pl.BlockSpec(memory_space=pltpu.SMEM)] + whole(4),
+        in_specs=whole(4),
         out_specs=whole(2),
         compiler_params=PARAMS,
         cost_estimate=cost(1 << 10),
         name="turn",
-    )(even, *operands)
-
-
-def near_kernel(even, keep, rest, zero, two, six, one, seven, above, below, far, own, other):
-    for target, parts in ((above, (one, zero, six)), (below, (seven, zero, two))):
+    )(*operands)
+
+
+def second_kernel(zero, two, six, above, below, far):
+    for target, parts in ((above, (zero, six)), (below, (zero, two))):
         for n, part in enumerate(parts):
             target[n * ROWS : (n + 1) * ROWS] = part[...]
-    share = jnp.full((ROWS, KW), even[0], F32) > 0.5
+    share = jnp.full((ROWS, KW), even_core().astype(F32)) > 0.5
     far[...] = jnp.where(share, six[...].astype(F32), two[...].astype(F32)).astype(BF16)
+
+
+def second_rows(*operands):
+    return pl.pallas_call(
+        second_kernel,
+        out_shape=shapes(*[((2 * ROWS, KW), BF16)] * 2, ((ROWS, KW), BF16)),
+        in_specs=whole(3),
+        out_specs=whole(3),
+        compiler_params=PARAMS,
+        cost_estimate=cost(1 << 10),
+        name="second_rows",
+    )(*operands)
+
+
+def keys_kernel(keep, first, rest, zero, two, six, below, above, far, own, other):
+    model = {0: zero[...], 2: two[...], 6: six[...], 4: far[...]}
+    model.update({1: below[:ROWS], 3: below[ROWS:], 7: above[:ROWS], 5: above[ROWS:]})
     total = jnp.zeros((TOK, KW), F32)
-    for n, ref in enumerate((two, six, zero)):
-        total += jnp.dot(rest[:, n * ROWS : (n + 1) * ROWS], ref[...], preferred_element_type=F32)
-    other[...] = total
+    for blocks, ref in ((FIRST, first), (REST, rest)):
+        for n, o in enumerate(blocks):
+            total += jnp.dot(ref[:, n * ROWS : (n + 1) * ROWS], model[o], preferred_element_type=F32)
+    other[...] = total.astype(BF16)
     total = jnp.zeros((TOK, KW), F32)
-    for n, ref in enumerate((two, six, zero), len(FIRST)):
-        total += jnp.dot(keep[:, n * ROWS : (n + 1) * ROWS], ref[...], preferred_element_type=F32)
-    own[...] = total
-
-
-def near_keys(even, *operands):
-    return pl.pallas_call(
-        near_kernel,
-        out_shape=shapes(
-            ((3 * ROWS, KW), BF16),
-            ((3 * ROWS, KW), BF16),
-            ((ROWS, KW), BF16),
-            ((TOK, KW), F32),
-            ((TOK, KW), F32),
-        ),
-        in_specs=[pl.BlockSpec(memory_space=pltpu.SMEM)] + whole(7),
-        out_specs=whole(5),
-        compiler_params=PARAMS,
-        cost_estimate=cost(1 << 10),
-        name="near_keys",
-    )(even, *operands)
-
-
-def keys_kernel(keep, first, below, above, far, near_own, near_other, own, other):
-    model = {1: below[ROWS : 2 * ROWS], 3: below[2 * ROWS :], 7: above[ROWS : 2 * ROWS], 5: above[2 * ROWS :]}
-    model[4] = far[...]
-    total = near_other[...]
-    for n, o in enumerate(FIRST):
-        total += jnp.dot(first[:, n * ROWS : (n + 1) * ROWS], model[o], preferred_element_type=F32)
-    other[...] = total.astype(BF16)
-    total = near_own[...]
-    for n, o in enumerate(FIRST):
+    for n, o in enumerate(FIRST + REST):
         total += jnp.dot(keep[:, n * ROWS : (n + 1) * ROWS], model[o], preferred_element_type=F32)
     own[...] = total
 
@@ -262,7 +271,7 @@
     return pl.pallas_call(
         keys_kernel,
         out_shape=shapes(((TOK, KW), F32), ((TOK, KW), BF16)),
-        in_specs=whole(7),
+        in_specs=whole(9),
         out_specs=whole(2),
         compiler_params=PARAMS,
         cost_estimate=cost(1 << 10),
@@ -291,7 +300,7 @@
 
 
 def ready_kernel(weight, own, above, below, numerator, first, second, near, shard, moment, square):
-    near[...] = own[2 * ROWS :] + above[:ROWS].astype(F32) + below[:ROWS].astype(F32)
+    near[...] = own[2 * ROWS :] + above[ROWS:].astype(F32) + below[ROWS:].astype(F32)
     shard[...] = numerator[0] * (0.5 - 0.5 * STEP_RATE * WEIGHT_DECAY / weight[0])
     moment[...] = BETA_ONE * first[0]
     square[...] = BETA_TWO * second[0]
@@ -336,12 +345,9 @@
     )(weight, sent, received)
 
 
-def push_by(distance, message, keys_operands, cosine, sine):
+def push_by(distance, message):
     n = lax.axis_size("rep")
-    received = lax.ppermute(message, "rep", [((i - distance) % n, i) for i in range(n)])
-    own_keys, other_keys = keys_parts(*keys_operands)
-    keys = finish_keys(own_keys, swap_x(other_keys), cosine, sine)
-    return received, keys
+    return lax.ppermute(message, "rep", [((i - distance) % n, i) for i in range(n)])
 
 
 def local(
@@ -356,50 +362,55 @@
     gossip_step,
 ):
     f = lax.axis_index("fsdp")
-    z, x = f // 2, f % 2
-    even = lax.axis_index("rep") % 2 == 0
-    place = jnp.stack([z, x]).astype(jnp.int32)
-
-    share = jnp.where(even, 1.0, 0.0).reshape(1).astype(F32)
-
-    send_first, scales = normalise_first(place, tokens, norm_gain, key_cotangent)
+    x = f % 2
+
+
+    send_first, scales, model = normalise_first(push_weight, tokens, norm_gain, key_cotangent, numerator)
     recv_first = swap_x(send_first)
-    other_ids = swap_x(lax.optimization_barrier((doc_ids, scales))[0])
-    pair_ids = jnp.concatenate([doc_ids[0], other_ids[0]])
-    documents = jnp.arange(DOCS, dtype=jnp.int32)[None, :]
-    counts = jnp.sum((pair_ids[:, None] == documents).astype(jnp.int32), axis=0, keepdims=True)
-    scales, counts = lax.optimization_barrier((scales, counts))
-    keep, send_rest, model = normalise(place, push_weight, tokens, norm_gain, scales, numerator)
-    behind_one, behind_two = along_z(counts, 1), along_z(counts, 2)
-    before = jnp.where(z >= 1, behind_one, 0) + jnp.where(z >= 2, behind_two, 0)
+    ids = jnp.broadcast_to(doc_ids[None], (2 * NZ, 1, TOK))
+    ids = lax.all_to_all(ids, "fsdp", 0, 0, tiled=True)
+    scales, ids, model = lax.optimization_barrier((scales, ids, model))
+    keep, send_rest = normalise(tokens, norm_gain, scales)
+    documents = jnp.arange(DOCS, dtype=jnp.int32)
+    totals = jnp.sum((ids.reshape(1, -1) == documents[:, None]).astype(jnp.int32), axis=1)
+    other = f + 1 - 2 * x
+    pair_ids = jnp.concatenate([doc_ids[0], lax.dynamic_index_in_dim(ids, other, 0, False)[0]])
     row = jnp.arange(TOK, dtype=jnp.int32)
-    index = jnp.concatenate([x * TOK + row, (1 - x) * TOK + row])
-    shift = jnp.where(pair_ids[:, None] == documents, before, 0)
-    shift = shift - jnp.where(pair_ids[:, None] > documents, counts, 0)
-    positions = index + jnp.sum(shift, axis=1)
+    index = jnp.concatenate([f * TOK + row, other * TOK + row])
+    starts = jnp.sum(jnp.where(pair_ids[:, None] > documents[None, :], totals[None, :], 0), axis=1)
+    positions = index - starts
     frequency = THETA ** (-(jnp.arange(HD // 2, dtype=jnp.float32) * 2.0 / HD))
     frequency = jnp.concatenate([frequency, frequency])
     angles = positions.astype(jnp.float32)[:, None] * frequency[None, :]
     cosine, sine = jnp.cos(angles), jnp.sin(angles)
 
-    three, one, five, seven, four, back = first_parts(keep, recv_first, key_cotangent, cosine, sine)
-    three, five, four = along_z(three, 1), along_z(five, -1), along_z_by_core(four, 2)
+    above, below, four, back = first_parts(keep, recv_first, key_cotangent, cosine, sine)
+    above, below, four = along_z(above, 1), along_z(below, -1), along_z_by_core(four, 2)
     recv_rest = swap_x(send_rest)
     six, two = along_z(model, 2), along_z(model, -2)
     own = rest_parts(keep, recv_rest, back)
-    above, below, far, near_own, near_other = near_keys(share, keep, recv_rest, model, two, six, one, seven)
-    above, below, far = along_z(above, 1), along_z(below, -1), along_z_by_core(far, 2)
-
-    up, down = turn(share, own, three, five, four)
+    model, six, two, own = lax.optimization_barrier((model, six, two, own))
+    rows_above, rows_below, far = second_rows(model, two, six)
+    rows_above, rows_below = along_z(rows_above, 1), along_z(rows_below, -1)
+    far = along_z_by_core(far, 2)
+
+    up, down = turn(own, above, below, four)
     up, down = along_z(up, 2), along_z(down, -2)
+
+    own_keys, other_keys = keys_parts(
+        keep, recv_first, recv_rest, model, two, six, rows_below, rows_above, far
+    )
+    other_recv = swap_x(other_keys)
 
     near = ready(push_weight, own, above, below, numerator, first_moment, second_moment)
     message, sent, first_new, second_new = step(push_weight, *near, up, down)
     bit_count = lax.axis_size("rep").bit_length() - 1
     branches = [partial(push_by, 1 << exponent) for exponent in range(bit_count)]
-    operands = (keep, recv_first, below, above, far, near_own, near_other)
-    received, keys = lax.switch(gossip_step[0] % bit_count, branches, message, operands, cosine, sine)
+    message = lax.optimization_barrier((message, other_keys))[0]
+    received = lax.switch(gossip_step[0] % bit_count, branches, message)
     numerator_new, weight_new = mix(push_weight, sent, received)
+    other_recv = lax.optimization_barrier((other_recv, received))[0]
+    keys = finish_keys(own_keys, other_recv, cosine, sine)
     return (keys, numerator_new, first_new, second_new, weight_new[0, :1])
 
 

time: 114 us -> 113 us (level)
  the two profiles are of different devices: /device:TPU:24 before, /device:TPU:128 now
where the time goes in v3:
time: 113 us; the launch traced here: 112 us
  starting transfers between devices  67.3 us (60%)
  Pallas kernels  15.7 us (14%)
  waiting for transfers between devices  15.5 us (14%)
  local copies, waits for them, and re-layouts  6.89 us (6%)
  other arithmetic  3.65 us (3%)
  between operations  2.38 us (2%)
    ppermute x8, starting transfers between devices, along_z(): return lax.ppermute(value, 'fsdp', route)  27 us
    ppermute x2, starting transfers between devices, along_z_by_core(): return lax.ppermute(value, ('rep', 'fsdp'), route)  12.9 us
    ppermute x3, starting transfers between devices, swap_x(): return lax.ppermute(value, 'fsdp', [(f, f ^ 1) for f in range(2 * NZ)])  10.1 us
    all_to_all x1, starting transfers between devices, local(): ids = lax.all_to_all(ids, 'fsdp', 0, 0, tiled=True)  10 us
    ppermute x1, waiting for transfers between devices, push_by(): lax.ppermute(message, 'rep', [((i - distance) % n, i) for i in range(n)])  9.56 us
    ppermute x1, starting transfers between devices, push_by(): lax.ppermute(message, 'rep', [((i - distance) % n, i) for i in range(n)])  7.22 us
    unnamed x36, local copies, waits for them, and re-layouts  5.38 us
    pallas_call x1, Pallas kernels, normalise_first(): pl.pallas_call(scale_kernel, out_shape=shapes(((TOK, len(FIRST) * ROWS +...  3.57 us
  transfers between devices with their start and end apart: 15, of which 4 were waited for; matrix products, arithmetic and copies ran while one was open for 4% of the time, Pallas kernels for 12%

profile of v3, /device:TPU:128, one launch (start us, length us, event | category | flops | bytes accessed | tf_op | source)
XLA Modules:
  0.0 112.3 jit_solution(2850267063163319373)
XLA Ops:
  0.6 0.0 copy-start.16
  0.7 1.4 %broadcast_in_dim.40 = s32[16,1,192]{2,1,0:T(1,128)} broadcast(s32[192]{0:T(256)} %bitcast.11), dimensions={2} | broadcast | bytes 13056 | tf_op jit(solution)/shard_map/broadcast_in_dim | solution.py:370
  2.1 10.0 %all-to-all-start = ((s32[16,1,192]{2,1,0:T(1,128)}), s32[16,1,192]{2,1,0:T(1,128)S(1)}, u32[]{:S(2)}, u32[]{:S(2)}) async-start(s32[16,1,192]{2,1,0:T(1,128)} %broadcast_in_dim.40), calls=%async_computation | async-start | bytes 32768 | tf_op jit(solution)/shard_map/all_to_all | solution.py:371
  12.7 0.0 copy-start.17
  12.7 3.6 %normalise_first.1 = (bf16[192,1792]{1,0:T(8,128)(2,1)}, f32[192,128]{1,0:T(8,128)}, bf16[256,512]{1,0:T(8,128)(2,1)}) custom-call(f32[1]{0:T(128)S(6)} %copy.19.weight, bf16[192,4096]{1,0:T(8,128)(2,1)} %tokens.3, f32[1,4096]{1,0:T(1,128)} %gain.3, bf16[192,512]{1,0:T(8,128)(2,1)} %cotangent.3, f32[1,256,512]{2,1,0:T(8,128)} %numerator.3), custom_call_target="tpu_custom_call" | custom-call | bytes 1024 | tf_op jit(solution)/shard_map/normalise_first/pallas_call | solution.py:119
  16.3 3.4 %collective-permute-start.5 = (bf16[192,1792]{1,0:T(8,128)(2,1)}, bf16[192,1792]{1,0:T(8,128)(2,1)S(1)}, u32[]{:S(2)}, u32[]{:S(2)}) collective-permute-start(bf16[192,1792]{1,0:T(8,128)(2,1)} %get-tuple-element.51), channel_id=1, source_target_pairs={{0,1},{1,0},{2,3},{3,2},{4,5},{5,4},{6,7},{7,6},{8,9},{9,8},{10,11... | collective-permute-start | bytes 2064392 | tf_op jit(solution)/shard_map/ppermute | solution.py:56
  19.7 0.1 pad_maximum_fusion
  19.8 5.5 %collective-permute-start.7 = (bf16[256,512]{1,0:T(8,128)(2,1)}, bf16[256,512]{1,0:T(8,128)(2,1)}, u32[]{:S(2)}, u32[]{:S(2)}) collective-permute-start(bf16[256,512]{1,0:T(8,128)(2,1)} %get-tuple-element.56.zero), channel_id=1, source_target_pairs={{0,4},{1,5},{2,6},{3,7},{4,8},{5,9},{6,10},{7,11},{8,12},{9,13},{1... | collective-permute-start | bytes 786440 | tf_op jit(solution)/shard_map/ppermute | solution.py:43
  25.3 1.9 %collective-permute-start.8 = (bf16[256,512]{1,0:T(8,128)(2,1)}, bf16[256,512]{1,0:T(8,128)(2,1)}, u32[]{:S(2)}, u32[]{:S(2)}) collective-permute-start(bf16[256,512]{1,0:T(8,128)(2,1)} %get-tuple-element.56.zero), channel_id=1, source_target_pairs={{0,12},{1,13},{2,14},{3,15},{4,0},{5,1},{6,2},{7,3},{8,4},{9,5},{1... | collective-permute-start | bytes 786440 | tf_op jit(solution)/shard_map/ppermute | solution.py:43
  27.2 0.9 copy-done.15
  28.1 1.8 %normalise.1 = (bf16[192,2048]{1,0:T(8,128)(2,1)S(1)}, bf16[192,768]{1,0:T(8,128)(2,1)}) custom-call(bf16[192,4096]{1,0:T(8,128)(2,1)S(1)} %copy-done, f32[1,4096]{1,0:T(1,128)S(1)} %copy-done.16, f32[192,128]{1,0:T(8,128)S(1)} %copy-done.15), custom_call_target="tpu_custom_call" | custom-call | bytes 1024 | tf_op jit(solution)/shard_map/normalise/pallas_call | solution.py:161
  29.9 2.5 %collective-permute-start.6 = (bf16[192,768]{1,0:T(8,128)(2,1)}, bf16[192,768]{1,0:T(8,128)(2,1)S(1)}, u32[]{:S(2)}, u32[]{:S(2)}) collective-permute-start(bf16[192,768]{1,0:T(8,128)(2,1)} %get-tuple-element.52), channel_id=1, source_target_pairs={{0,1},{1,0},{2,3},{3,2},{4,5},{5,4},{6,7},{7,6},{8,9},{9,8},{10,11... | collective-permute-start | bytes 884744 | tf_op jit(solution)/shard_map/ppermute | solution.py:56
  32.4 0.1 pad_add_fusion
  32.5 0.1 eq.18
  32.6 0.1 convert_reduce_fusion
  32.7 0.1 select_reduce_fusion
  32.8 0.1 fusion.5
  32.9 0.8 multiply_sine_fusion
  33.7 3.0 %collective-permute-done.5.recv.first = bf16[192,1792]{1,0:T(8,128)(2,1)S(1)} collective-permute-done((bf16[192,1792]{1,0:T(8,128)(2,1)}, bf16[192,1792]{1,0:T(8,128)(2,1)S(1)}, u32[]{:S(2)}, u32[]{:S(2)}) %collective-permute-start.5) | collective-permute-done | bytes 688160 | tf_op jit(solution)/shard_map/ppermute | solution.py:56
  36.7 0.9 copy-done.10
  37.6 1.3 %first_parts.1 = (bf16[512,512]{1,0:T(8,128)(2,1)S(1)}, bf16[512,512]{1,0:T(8,128)(2,1)S(1)}, bf16[256,512]{1,0:T(8,128)(2,1)S(1)}, bf16[384,512]{1,0:T(8,128)(2,1)S(1)}) custom-call(bf16[192,2048]{1,0:T(8,128)(2,1)S(1)} %get-tuple-element.50.keep, bf16[192,1792]{1,0:T(8,128)(2,1)S(1)} %collective-permute-done.5.recv.first, bf16[192,512]{1,0:T(8,128)(2,1)S(1)} %copy-done.10, ...), custom_call_target="tpu_custom_call" | custom-call | bytes 1024 | tf_op jit(solution)/shard_map/first_parts/pallas_call | solution.py:199
  38.9 3.5 %collective-permute-start.13 = (bf16[512,512]{1,0:T(8,128)(2,1)S(1)}, bf16[512,512]{1,0:T(8,128)(2,1)S(1)}, u32[]{:S(2)}, u32[]{:S(2)}) collective-permute-start(bf16[512,512]{1,0:T(8,128)(2,1)S(1)} %get-tuple-element.65), channel_id=1, source_target_pairs={{0,2},{1,3},{2,4},{3,5},{4,6},{5,7},{6,8},{7,9},{8,10},{9,11},{10,... | collective-permute-start | bytes 1572872 | tf_op jit(solution)/shard_map/ppermute | solution.py:43
  42.4 2.4 %collective-permute-start.14 = (bf16[512,512]{1,0:T(8,128)(2,1)S(1)}, bf16[512,512]{1,0:T(8,128)(2,1)S(1)}, u32[]{:S(2)}, u32[]{:S(2)}) collective-permute-start(bf16[512,512]{1,0:T(8,128)(2,1)S(1)} %get-tuple-element.66), channel_id=1, source_target_pairs={{0,14},{1,15},{2,0},{3,1},{4,2},{5,3},{6,4},{7,5},{8,6},{9,7},{10,... | collective-permute-start | bytes 1572872 | tf_op jit(solution)/shard_map/ppermute | solution.py:43
  44.8 0.4 fusion.2
  45.2 0.7 copy-done.6
  45.9 0.4 convolution_add_fusion.own
  46.3 6.4 %collective-permute-start.15 = (bf16[256,512]{1,0:T(8,128)(2,1)S(1)}, bf16[256,512]{1,0:T(8,128)(2,1)S(1)}, u32[]{:S(2)}, u32[]{:S(2)}) collective-permute-start(bf16[256,512]{1,0:T(8,128)(2,1)S(1)} %get-tuple-element.70), channel_id=1, source_target_pairs={{0,4},{1,5},{2,6},{3,7},{4,8},{5,9},{6,10},{7,11},{8,12},{9,13},{1... | collective-permute-start | bytes 786440 | tf_op jit(solution)/shard_map/ppermute | solution.py:52
  52.8 2.1 %second_rows.1 = (bf16[512,512]{1,0:T(8,128)(2,1)}, bf16[512,512]{1,0:T(8,128)(2,1)}, bf16[256,512]{1,0:T(8,128)(2,1)}) custom-call(bf16[256,512]{1,0:T(8,128)(2,1)S(1)} %copy-done.8, bf16[256,512]{1,0:T(8,128)(2,1)} %collective-permute-done.8.two, bf16[256,512]{1,0:T(8,128)(2,1)} %collective-permute-done.7.six), custom_call_target="tpu_custom_call" | custom-call | bytes 1024 | tf_op jit(solution)/shard_map/second_rows/pallas_call | solution.py:245
  54.9 1.9 %collective-permute-start.9 = (bf16[512,512]{1,0:T(8,128)(2,1)}, bf16[512,512]{1,0:T(8,128)(2,1)}, u32[]{:S(2)}, u32[]{:S(2)}) collective-permute-start(bf16[512,512]{1,0:T(8,128)(2,1)} %get-tuple-element.59), channel_id=1, source_target_pairs={{0,14},{1,15},{2,0},{3,1},{4,2},{5,3},{6,4},{7,5},{8,6},{9,7},{10,... | collective-permute-start | bytes 1572872 | tf_op jit(solution)/shard_map/ppermute | solution.py:43
  56.8 3.9 %collective-permute-start.10 = (bf16[512,512]{1,0:T(8,128)(2,1)}, bf16[512,512]{1,0:T(8,128)(2,1)}, u32[]{:S(2)}, u32[]{:S(2)}) collective-permute-start(bf16[512,512]{1,0:T(8,128)(2,1)} %get-tuple-element.60), channel_id=1, source_target_pairs={{0,2},{1,3},{2,4},{3,5},{4,6},{5,7},{6,8},{7,9},{8,10},{9,11},{10,... | collective-permute-start | bytes 1572872 | tf_op jit(solution)/shard_map/ppermute | solution.py:43
  60.8 0.2 collective-permute-done.15.four
  60.9 6.5 %collective-permute-start.11 = (bf16[256,512]{1,0:T(8,128)(2,1)}, bf16[256,512]{1,0:T(8,128)(2,1)}, u32[]{:S(2)}, u32[]{:S(2)}) collective-permute-start(bf16[256,512]{1,0:T(8,128)(2,1)} %get-tuple-element.61), channel_id=1, source_target_pairs={{0,4},{1,5},{2,6},{3,7},{4,8},{5,9},{6,10},{7,11},{8,12},{9,13},{1... | collective-permute-start | bytes 786440 | tf_op jit(solution)/shard_map/ppermute | solution.py:52
  67.5 1.0 turn.1
  68.5 0.8 copy-done.2
  69.2 1.9 %collective-permute-start.17 = (bf16[256,512]{1,0:T(8,128)(2,1)}, bf16[256,512]{1,0:T(8,128)(2,1)}, u32[]{:S(2)}, u32[]{:S(2)}) collective-permute-start(bf16[256,512]{1,0:T(8,128)(2,1)} %get-tuple-element.72), channel_id=1, source_target_pairs={{0,12},{1,13},{2,14},{3,15},{4,0},{5,1},{6,2},{7,3},{8,4},{9,5},{1... | collective-permute-start | bytes 786440 | tf_op jit(solution)/shard_map/ppermute | solution.py:43
  71.2 6.0 %collective-permute-start.16 = (bf16[256,512]{1,0:T(8,128)(2,1)}, bf16[256,512]{1,0:T(8,128)(2,1)}, u32[]{:S(2)}, u32[]{:S(2)}) collective-permute-start(bf16[256,512]{1,0:T(8,128)(2,1)} %get-tuple-element.71), channel_id=1, source_target_pairs={{0,4},{1,5},{2,6},{3,7},{4,8},{5,9},{6,10},{7,11},{8,12},{9,13},{1... | collective-permute-start | bytes 786440 | tf_op jit(solution)/shard_map/ppermute | solution.py:43
  78.0 1.1 copy-done.7
  79.0 0.9 copy-done.9
  80.0 3.0 %keys_parts.1 = (f32[192,512]{1,0:T(8,128)S(1)}, bf16[192,512]{1,0:T(8,128)(2,1)}) custom-call(bf16[192,2048]{1,0:T(8,128)(2,1)S(1)} %get-tuple-element.50.keep, bf16[192,1792]{1,0:T(8,128)(2,1)S(1)} %collective-permute-done.5.recv.first, bf16[192,768]{1,0:T(8,128)(2,1)S(1)} %copy-done.7, bf16[256,512]{1,0:T(8,128)(2,1)S(1)} %copy-done.9, ...), custom_call_target="tpu_custom_call" | custom-call | bytes 1024 | tf_op jit(solution)/shard_map/keys_parts/pallas_call | solution.py:271
  82.9 4.3 %collective-permute-start.12 = (bf16[192,512]{1,0:T(8,128)(2,1)}, bf16[192,512]{1,0:T(8,128)(2,1)S(1)}, u32[]{:S(2)}, u32[]{:S(2)}) collective-permute-start(bf16[192,512]{1,0:T(8,128)(2,1)} %get-tuple-element.63), channel_id=1, source_target_pairs={{0,1},{1,0},{2,3},{3,2},{4,5},{5,4},{6,7},{7,6},{8,9},{9,8},{10,11... | collective-permute-start | bytes 589832 | tf_op jit(solution)/shard_map/ppermute | solution.py:56
  87.3 0.2 ready.1
  87.5 2.8 %collective-permute-done.17 = bf16[256,512]{1,0:T(8,128)(2,1)} collective-permute-done((bf16[256,512]{1,0:T(8,128)(2,1)}, bf16[256,512]{1,0:T(8,128)(2,1)}, u32[]{:S(2)}, u32[]{:S(2)}) %collective-permute-start.17) | collective-permute-done | bytes 262176 | tf_op jit(solution)/shard_map/ppermute | solution.py:43
  90.3 2.4 %fusion.8 = (bf16[256,512]{1,0:T(8,128)(2,1)S(1)}, f32[256,512]{1,0:T(8,128)S(1)}, f32[1,256,512]{2,1,0:T(8,128)}, f32[1,256,512]{2,1,0:T(8,128)}) fusion(f32[256,512]{1,0:T(8,128)S(1)} %get-tuple-element.67, f32[256,512]{1,0:T(8,128)S(1)} %get-tuple-element.73, f32[256,512]{1,0:T(8,128)S(1)} %get-tuple-element.68, ...), kind=kLoop, calls=%fused_computation.26 | loop fusion | flops 1966080 | bytes 4456448 | tf_op jit(solution)/shard_map/convert
  92.7 16.8 %conditional.1 = (bf16[272,512]{1,0:T(8,128)(2,1)}) conditional(s32[]{:T(128)} %clamp.3, bf16[272,512]{1,0:T(8,128)(2,1)S(1)} %concatenate.19, bf16[272,512]{1,0:T(8,128)(2,1)S(1)} %concatenate.19, bf16[272,512]{1,0:T(8,128)(2,1)S(1)} %concatenate.19, bf16[272,512]{1,0:T(8,128)(2,1)S(1)} %concatenate.19, ...), branch_computations={%region_2.3_spmd, %region_3.4_spmd, %region_4.5_spmd, %region_5.6_... | conditional | bytes 1114160 | solution.py:410
  92.7 7.2 %collective-permute-start = (bf16[272,512]{1,0:T(8,128)(2,1)S(1)}, bf16[272,512]{1,0:T(8,128)(2,1)}, u32[]{:S(2)}, u32[]{:S(2)}) collective-permute-start(bf16[272,512]{1,0:T(8,128)(2,1)S(1)} %param), channel_id=1, source_target_pairs={{496,0},{0,16},{16,32},{32,48},{48,64},{64,80},{80,96},{96,112},{1... | collective-permute-start | bytes 835592 | tf_op jit(solution)/shard_map/cond/branch_0_fun/ppermute | solution.py:350
  99.9 9.6 %collective-permute-done = bf16[272,512]{1,0:T(8,128)(2,1)} collective-permute-done((bf16[272,512]{1,0:T(8,128)(2,1)S(1)}, bf16[272,512]{1,0:T(8,128)(2,1)}, u32[]{:S(2)}, u32[]{:S(2)}) %collective-permute-start) | collective-permute-done | bytes 278560 | tf_op jit(solution)/shard_map/cond/branch_0_fun/ppermute | solution.py:350
  109.5 1.8 %mix.1 = (f32[1,256,512]{2,1,0:T(8,128)}, f32[1,128]{1,0:T(1,128)}) custom-call(f32[1]{0:T(128)S(6)} %copy.19.weight, f32[256,512]{1,0:T(8,128)S(1)} %get-tuple-element.79.sent, bf16[272,512]{1,0:T(8,128)(2,1)} %get-tuple-element.86.received), custom_call_target="tpu_custom_call" | custom-call | bytes 1024 | tf_op jit(solution)/shard_map/mix/pallas_call | solution.py:337
  111.3 1.0 finish_keys.1
  (44 shorter events, 0.2 us)
Async XLA Ops:
  0.6 26.6 %copy-start = (bf16[192,4096]{1,0:T(8,128)(2,1)S(1)}, bf16[192,4096]{1,0:T(8,128)(2,1)}, u32[]{:S(2)}) copy-start(bf16[192,4096]{1,0:T(8,128)(2,1)} %tokens.3) | copy-start | bytes 4718596
  0.6 26.6 %copy-start.16 = (f32[1,4096]{1,0:T(1,128)S(1)}, f32[1,4096]{1,0:T(1,128)}, u32[]{:S(2)}) copy-start(f32[1,4096]{1,0:T(1,128)} %gain.3) | copy-start | bytes 49156
  2.1 17.7 %all-to-all-start = ((s32[16,1,192]{2,1,0:T(1,128)}), s32[16,1,192]{2,1,0:T(1,128)S(1)}, u32[]{:S(2)}, u32[]{:S(2)}) async-start(s32[16,1,192]{2,1,0:T(1,128)} %broadcast_in_dim.40), calls=%async_computation | async-start | bytes 32768 | tf_op jit(solution)/shard_map/all_to_all | solution.py:371
  12.7 19.7 %copy-start.17 = (s32[1,192]{1,0:T(1,128)S(1)}, s32[1,192]{1,0:T(1,128)}, u32[]{:S(2)}) copy-start(s32[1,192]{1,0:T(1,128)} %param.16) | copy-start | bytes 2308
  16.3 20.4 %collective-permute-start.5 = (bf16[192,1792]{1,0:T(8,128)(2,1)}, bf16[192,1792]{1,0:T(8,128)(2,1)S(1)}, u32[]{:S(2)}, u32[]{:S(2)}) collective-permute-start(bf16[192,1792]{1,0:T(8,128)(2,1)} %get-tuple-element.51), channel_id=1, source_target_pairs={{0,1},{1,0},{2,3},{3,2},{4,5},{5,4},{6,7},{7,6},{8,9},{9,8},{10,11... | collective-permute-start | bytes 2064392 | tf_op jit(solution)/shard_map/ppermute | solution.py:56
  19.8 26.5 %collective-permute-start.7 = (bf16[256,512]{1,0:T(8,128)(2,1)}, bf16[256,512]{1,0:T(8,128)(2,1)}, u32[]{:S(2)}, u32[]{:S(2)}) collective-permute-start(bf16[256,512]{1,0:T(8,128)(2,1)} %get-tuple-element.56.zero), channel_id=1, source_target_pairs={{0,4},{1,5},{2,6},{3,7},{4,8},{5,9},{6,10},{7,11},{8,12},{9,13},{1... | collective-permute-start | bytes 786440 | tf_op jit(solution)/shard_map/ppermute | solution.py:43
  25.3 21.0 %collective-permute-start.8 = (bf16[256,512]{1,0:T(8,128)(2,1)}, bf16[256,512]{1,0:T(8,128)(2,1)}, u32[]{:S(2)}, u32[]{:S(2)}) collective-permute-start(bf16[256,512]{1,0:T(8,128)(2,1)} %get-tuple-element.56.zero), channel_id=1, source_target_pairs={{0,12},{1,13},{2,14},{3,15},{4,0},{5,1},{6,2},{7,3},{8,4},{9,5},{1... | collective-permute-start | bytes 786440 | tf_op jit(solution)/shard_map/ppermute | solution.py:43
  27.2 0.9 copy-start.15
  29.9 14.9 %collective-permute-start.6 = (bf16[192,768]{1,0:T(8,128)(2,1)}, bf16[192,768]{1,0:T(8,128)(2,1)S(1)}, u32[]{:S(2)}, u32[]{:S(2)}) collective-permute-start(bf16[192,768]{1,0:T(8,128)(2,1)} %get-tuple-element.52), channel_id=1, source_target_pairs={{0,1},{1,0},{2,3},{3,2},{4,5},{5,4},{6,7},{7,6},{8,9},{9,8},{10,11... | collective-permute-start | bytes 884744 | tf_op jit(solution)/shard_map/ppermute | solution.py:56
  36.7 0.9 copy-start.10
  38.9 28.5 %collective-permute-start.13 = (bf16[512,512]{1,0:T(8,128)(2,1)S(1)}, bf16[512,512]{1,0:T(8,128)(2,1)S(1)}, u32[]{:S(2)}, u32[]{:S(2)}) collective-permute-start(bf16[512,512]{1,0:T(8,128)(2,1)S(1)} %get-tuple-element.65), channel_id=1, source_target_pairs={{0,2},{1,3},{2,4},{3,5},{4,6},{5,7},{6,8},{7,9},{8,10},{9,11},{10,... | collective-permute-start | bytes 1572872 | tf_op jit(solution)/shard_map/ppermute | solution.py:43
  42.4 25.0 %collective-permute-start.14 = (bf16[512,512]{1,0:T(8,128)(2,1)S(1)}, bf16[512,512]{1,0:T(8,128)(2,1)S(1)}, u32[]{:S(2)}, u32[]{:S(2)}) collective-permute-start(bf16[512,512]{1,0:T(8,128)(2,1)S(1)} %get-tuple-element.66), channel_id=1, source_target_pairs={{0,14},{1,15},{2,0},{3,1},{4,2},{5,3},{6,4},{7,5},{8,6},{9,7},{10,... | collective-permute-start | bytes 1572872 | tf_op jit(solution)/shard_map/ppermute | solution.py:43
  45.2 0.7 copy-start.6
  45.9 6.9 %copy-start.8 = (bf16[256,512]{1,0:T(8,128)(2,1)S(1)}, bf16[256,512]{1,0:T(8,128)(2,1)}, u32[]{:S(2)}) copy-start(bf16[256,512]{1,0:T(8,128)(2,1)} %get-tuple-element.56.zero) | copy-start | bytes 786436
  46.3 14.6 %collective-permute-start.15 = (bf16[256,512]{1,0:T(8,128)(2,1)S(1)}, bf16[256,512]{1,0:T(8,128)(2,1)S(1)}, u32[]{:S(2)}, u32[]{:S(2)}) collective-permute-start(bf16[256,512]{1,0:T(8,128)(2,1)S(1)} %get-tuple-element.70), channel_id=1, source_target_pairs={{0,4},{1,5},{2,6},{3,7},{4,8},{5,9},{6,10},{7,11},{8,12},{9,13},{1... | collective-permute-start | bytes 786440 | tf_op jit(solution)/shard_map/ppermute | solution.py:52
  54.9 23.0 %collective-permute-start.9 = (bf16[512,512]{1,0:T(8,128)(2,1)}, bf16[512,512]{1,0:T(8,128)(2,1)}, u32[]{:S(2)}, u32[]{:S(2)}) collective-permute-start(bf16[512,512]{1,0:T(8,128)(2,1)} %get-tuple-element.59), channel_id=1, source_target_pairs={{0,14},{1,15},{2,0},{3,1},{4,2},{5,3},{6,4},{7,5},{8,6},{9,7},{10,... | collective-permute-start | bytes 1572872 | tf_op jit(solution)/shard_map/ppermute | solution.py:43
  56.8 21.1 %collective-permute-start.10 = (bf16[512,512]{1,0:T(8,128)(2,1)}, bf16[512,512]{1,0:T(8,128)(2,1)}, u32[]{:S(2)}, u32[]{:S(2)}) collective-permute-start(bf16[512,512]{1,0:T(8,128)(2,1)} %get-tuple-element.60), channel_id=1, source_target_pairs={{0,2},{1,3},{2,4},{3,5},{4,6},{5,7},{6,8},{7,9},{8,10},{9,11},{10,... | collective-permute-start | bytes 1572872 | tf_op jit(solution)/shard_map/ppermute | solution.py:43
  60.9 17.0 %collective-permute-start.11 = (bf16[256,512]{1,0:T(8,128)(2,1)}, bf16[256,512]{1,0:T(8,128)(2,1)}, u32[]{:S(2)}, u32[]{:S(2)}) collective-permute-start(bf16[256,512]{1,0:T(8,128)(2,1)} %get-tuple-element.61), channel_id=1, source_target_pairs={{0,4},{1,5},{2,6},{3,7},{4,8},{5,9},{6,10},{7,11},{8,12},{9,13},{1... | collective-permute-start | bytes 786440 | tf_op jit(solution)/shard_map/ppermute | solution.py:52
  67.5 1.0 copy-start.4
  68.5 0.8 copy-start.2
  69.2 21.0 %collective-permute-start.17 = (bf16[256,512]{1,0:T(8,128)(2,1)}, bf16[256,512]{1,0:T(8,128)(2,1)}, u32[]{:S(2)}, u32[]{:S(2)}) collective-permute-start(bf16[256,512]{1,0:T(8,128)(2,1)} %get-tuple-element.72), channel_id=1, source_target_pairs={{0,12},{1,13},{2,14},{3,15},{4,0},{5,1},{6,2},{7,3},{8,4},{9,5},{1... | collective-permute-start | bytes 786440 | tf_op jit(solution)/shard_map/ppermute | solution.py:43
  71.2 19.1 %collective-permute-start.16 = (bf16[256,512]{1,0:T(8,128)(2,1)}, bf16[256,512]{1,0:T(8,128)(2,1)}, u32[]{:S(2)}, u32[]{:S(2)}) collective-permute-start(bf16[256,512]{1,0:T(8,128)(2,1)} %get-tuple-element.71), channel_id=1, source_target_pairs={{0,4},{1,5},{2,6},{3,7},{4,8},{5,9},{6,10},{7,11},{8,12},{9,13},{1... | collective-permute-start | bytes 786440 | tf_op jit(solution)/shard_map/ppermute | solution.py:43
  77.9 9.4 %copy-start.1 = (f32[1,256,512]{2,1,0:T(8,128)S(1)}, f32[1,256,512]{2,1,0:T(8,128)}, u32[]{:S(2)}) copy-start(f32[1,256,512]{2,1,0:T(8,128)} %numerator.3) | copy-start | bytes 1572868
  77.9 9.4 %copy-start.3 = (bf16[512,512]{1,0:T(8,128)(2,1)S(1)}, bf16[512,512]{1,0:T(8,128)(2,1)}, u32[]{:S(2)}) copy-start(bf16[512,512]{1,0:T(8,128)(2,1)} %copy-done.2) | copy-start | bytes 1572868
  77.9 9.4 %copy-start.5 = (bf16[512,512]{1,0:T(8,128)(2,1)S(1)}, bf16[512,512]{1,0:T(8,128)(2,1)}, u32[]{:S(2)}) copy-start(bf16[512,512]{1,0:T(8,128)(2,1)} %copy-done.4) | copy-start | bytes 1572868
  77.9 1.1 copy-start.7
  79.0 0.9 copy-start.9
  80.0 7.3 %copy-start.11 = (f32[1,256,512]{2,1,0:T(8,128)S(1)}, f32[1,256,512]{2,1,0:T(8,128)}, u32[]{:S(2)}) copy-start(f32[1,256,512]{2,1,0:T(8,128)} %first.1) | copy-start | bytes 1572868
  80.0 7.3 %copy-start.12 = (f32[1,256,512]{2,1,0:T(8,128)S(1)}, f32[1,256,512]{2,1,0:T(8,128)}, u32[]{:S(2)}) copy-start(f32[1,256,512]{2,1,0:T(8,128)} %second.1) | copy-start | bytes 1572868
  82.9 4.6 %copy-start.13 = (f32[192,512]{1,0:T(8,128)}, f32[192,512]{1,0:T(8,128)S(1)}, u32[]{:S(2)}) copy-start(f32[192,512]{1,0:T(8,128)S(1)} %get-tuple-element.62.own) | copy-start | bytes 1179652
  82.9 26.6 %collective-permute-start.12 = (bf16[192,512]{1,0:T(8,128)(2,1)}, bf16[192,512]{1,0:T(8,128)(2,1)S(1)}, u32[]{:S(2)}, u32[]{:S(2)}) collective-permute-start(bf16[192,512]{1,0:T(8,128)(2,1)} %get-tuple-element.63), channel_id=1, source_target_pairs={{0,1},{1,0},{2,3},{3,2},{4,5},{5,4},{6,7},{7,6},{8,9},{9,8},{10,11... | collective-permute-start | bytes 589832 | tf_op jit(solution)/shard_map/ppermute | solution.py:56
  92.7 18.6 %copy-start.14 = (f32[192,512]{1,0:T(8,128)S(1)}, f32[192,512]{1,0:T(8,128)}, u32[]{:S(2)}) copy-start(f32[192,512]{1,0:T(8,128)} %copy-done.13) | copy-start | bytes 1179652
  92.7 16.8 %collective-permute-start = (bf16[272,512]{1,0:T(8,128)(2,1)S(1)}, bf16[272,512]{1,0:T(8,128)(2,1)}, u32[]{:S(2)}, u32[]{:S(2)}) collective-permute-start(bf16[272,512]{1,0:T(8,128)(2,1)S(1)} %param), channel_id=1, source_target_pairs={{496,0},{0,16},{16,32},{32,48},{48,64},{64,80},{80,96},{96,112},{1... | collective-permute-start | bytes 835592 | tf_op jit(solution)/shard_map/cond/branch_0_fun/ppermute | solution.py:350
